TPU v7x, 256 devices: a whole 4x4x8 slice. The times are simulated.
256 devices in a mesh: rows: 32 (over x, y, z_lo), chan: 8 (over z_hi, core).
Axes of the slice: x: 4, y: 4, z: 8 (z_hi: 4, z_lo: 2; z = z_hi * 2 + z_lo), core: 2. Of those that a mesh axis runs over, the one named last changes fastest.
Arguments:
- frame_adjoint: bfloat16 [32, 192, 32, 128], P('rows', 'chan'), may hold values from -6 to 6
- frame_slot: int32 [32], replicated, may hold values from 0 to 31, each once
- inputs: bfloat16 [32, 192, 32, 128], P(None, 'chan', 'rows')
- gain: float32 [192], P('chan'), may hold values from 0.1 to 1.9
- weight: bfloat16 [27, 192, 192], P(None, 'chan'), may hold values from -0.078125 to 0.078125
Outputs:
- input_adjoint: bfloat16 [32, 192, 32, 128], P(None, 'chan', 'rows')
- weight_adjoint: float32 [27, 192, 192], P(None, 'chan')
Inputs may be any that keep to these rules, and one draw needn't show every extreme that they name: `frame_slot`: each frame appears in exactly one slot.
All inputs are finite; a program needn't handle non-finite values.
Results may differ from a plain program's by a relative error of at most 0.003.
Values may be sent and summed in bfloat16 or wider, within the bound.
A program may use at most 128 MiB of HBM per device.

v0:
```python
import jax
import jax.numpy as jnp
from jax import lax
from jax.sharding import PartitionSpec as P

CHANNELS = 192


epsilon = 1e-06


def extended(block, sides, width):
    for axis, dim in sides:
        count = lax.axis_size(axis)
        forward = [(i, i + 1) for i in range(count - 1)]
        backward = [(target, source) for source, target in forward]
        low = lax.ppermute(
            lax.slice_in_dim(block, block.shape[dim] - width, None, axis=dim), axis, forward
        )
        high = lax.ppermute(lax.slice_in_dim(block, 0, width, axis=dim), axis, backward)
        block = jnp.concatenate([low, block, high], axis=dim)
    return block


def transpose_conv(padded, kernel, frames, rows, width):
    summed = jnp.zeros((frames, kernel.shape[2], rows, width), jnp.float32)
    for frame_off in range(3):
        windows = []
        for row_off in range(3):
            for col_off in range(3):
                windows.append(
                    padded[
                        2 - frame_off : 2 - frame_off + frames,
                        :,
                        2 - row_off : 2 - row_off + rows,
                        2 - col_off : 2 - col_off + width,
                    ]
                )
        stacked = jnp.stack(windows)
        taps = kernel[frame_off * 9 : frame_off * 9 + 9]
        summed = summed + jnp.einsum(
            "kforw,koc->fcrw", stacked, taps, preferred_element_type=jnp.float32
        )
    return summed


def kernel_grad(adjoint, padded, frames, rows, width):
    grad_list = []
    for frame_off in range(3):
        windows = []
        for row_off in range(3):
            for col_off in range(3):
                windows.append(
                    padded[
                        frame_off : frame_off + frames,
                        :,
                        row_off : row_off + rows,
                        col_off : col_off + width,
                    ]
                )
        stacked = jnp.stack(windows)
        grad_list.append(
            jnp.einsum("forw,kfcrw->koc", adjoint, stacked, preferred_element_type=jnp.float32)
        )
    return jnp.concatenate(grad_list, axis=0)


def shards(frame_adjoint, frame_slot, inputs, gain, weight):
    arrived = lax.all_to_all(frame_adjoint, "rows", split_axis=2, concat_axis=0, tiled=True)
    frames = arrived.shape[0]
    rows = arrived.shape[2]
    width = arrived.shape[3]
    onehot = (frame_slot[None, :] == jnp.arange(frames, dtype=jnp.int32)[:, None]).astype(
        jnp.bfloat16
    )
    adjoint = jnp.einsum(
        "tj,jcrw->tcrw", onehot, arrived, preferred_element_type=jnp.float32
    ).astype(jnp.bfloat16)
    values = inputs.astype(jnp.float32)
    squares = lax.psum(jnp.sum(values * values, axis=1), "chan")
    scale = lax.rsqrt(squares / CHANNELS + epsilon)[:, None]
    normed = values * scale * gain[None, :, None, None]
    sigma = jax.nn.sigmoid(normed)
    hidden = (normed * sigma).astype(jnp.bfloat16)
    hidden_rim = extended(hidden, (("rows", 2),), 1)
    hidden_pad = jnp.pad(hidden_rim, ((2, 0), (0, 0), (0, 0), (1, 1)))
    adjoint_rim = extended(adjoint, (("rows", 2),), 1)
    adjoint_pad = jnp.pad(adjoint_rim, ((0, 2), (0, 0), (0, 0), (1, 1)))
    factor = float(frames * rows * lax.axis_size("rows") * width) ** (-0.5)
    local_grad = (
        kernel_grad(
            adjoint, lax.all_gather(hidden_pad, "chan", axis=1, tiled=True), frames, rows, width
        )
        * factor
    )
    partial_sum = transpose_conv(adjoint_pad, weight, frames, rows, width)
    hidden_adjoint = lax.psum_scatter(partial_sum, "chan", scatter_dimension=1, tiled=True)
    weight_adjoint = lax.psum(local_grad, "rows")
    normed_adjoint = (
        hidden_adjoint * sigma * (1.0 + normed * (1.0 - sigma)) * gain[None, :, None, None]
    )
    projection = lax.psum(jnp.sum(normed_adjoint * values, axis=1), "chan")[:, None]
    input_adjoint = scale * normed_adjoint - values * scale * scale * scale * projection / CHANNELS
    return (input_adjoint.astype(jnp.bfloat16), weight_adjoint)


def solution(mesh):
    in_specs = (
        P("rows", "chan", None, None),
        P(),
        P(None, "chan", "rows", None),
        P("chan"),
        P(None, "chan", None),
    )
    out_specs = (P(None, "chan", "rows", None), P(None, "chan", None))
    return jax.shard_map(shards, mesh=mesh, in_specs=in_specs, out_specs=out_specs, check_vma=False)
```

profile of v0, /device:TPU:8, one launch (start us, length us, event | category | flops | bytes accessed | tf_op | source)
XLA Modules:
  0.0 604.2 jit_solution(9993146138802715559)
XLA Ops:
  7.2 1.0 copy.16
  8.2 16.5 %all_to_all.15 = bf16[1,24,32,128]{3,1,0,2:T(8,128)(2,1)S(1)} all-to-all(bf16[1,24,32,128]{3,1,0,2:T(8,128)(2,1)S(1)} %copy.16), channel_id=1, replica_groups=mesh['rows'=32,'chan'=8] {'rows'}, dimensions={2} | all-to-all | bytes 393216 | tf_op jit(solution)/shard_map/all_to_all | solution.py:69
  24.8 0.8 convolution_convert_fusion
  25.6 3.5 collective-permute-start.1
  29.1 2.4 collective-permute-start
  31.5 3.2 collective-permute-done.1
  34.6 3.6 collective-permute-done
  38.3 0.6 fusion.51
  38.9 0.3 fusion.111
  39.1 0.3 fusion.110
  39.4 0.1 fusion.109
  39.6 0.4 fusion.93
  40.0 0.3 fusion.92
  40.4 0.2 fusion.91
  40.6 0.3 fusion.90
  41.0 0.4 fusion.89
  41.4 0.2 fusion.88
  41.6 0.8 fusion.18
  42.4 0.8 fusion.20
  43.3 2.9 fusion.6
  46.2 0.8 copy-done.1
  47.2 33.2 %psum.21 = f32[32,1,128]{2,0,1:T(8,128)S(1)} all-reduce(f32[32,1,128]{2,0,1:T(8,128)S(1)} %bitcast.312), channel_id=1, replica_groups=mesh['rows'=32,'chan'=8] {'chan'}, use_global_device_ids=true, to_apply=%region_1.0 | all-reduce | flops 4096 | bytes 32768 | tf_op jit(solution)/shard_map/psum | solution.py:80
  80.4 14.0 %reduce-scatter.2.cloned.1.call-done = f32[32,24,1,128]{3,1,0,2:T(8,128)} async-done(((f32[32,192,1,128]{3,1,0,2:T(8,128)}), f32[32,24,1,128]{3,1,0,2:T(8,128)}) %reduce-scatter.2.cloned.1.call-update) | async-done | bytes 393232 | tf_op jit(solution)/shard_map/reduce_scatter | solution.py:97
  94.4 1.3 fusion.79
  95.7 4.3 collective-permute-start.3
  100.0 2.8 collective-permute-start.2
  102.8 3.7 collective-permute-done.3
  106.5 5.2 collective-permute-done.2
  111.7 1.6 fusion.56
  113.4 0.2 all-reduce.4.cloned.1.call-start
  113.6 89.1 %all-gather.2.cloned.1.call-done = bf16[34,192,3,130]{3,1,0,2:T(8,128)(2,1)} async-done(((bf16[34,24,3,130]{3,1,0,2:T(8,128)(2,1)}), bf16[34,192,3,130]{3,1,0,2:T(8,128)(2,1)}) %all-gather.2.cloned.1.call-update) | async-done | bytes 5091856 | tf_op jit(solution)/shard_map/all_gather | solution.py:92
  202.8 4.6 fusion.48
  207.3 8.0 %fusion.47 = (bf16[9,32,192,1,128]{4,2,1,3,0:T(8,128)(2,1)S(1)}, bf16[9,32,192,1,128]{4,2,1,3,0:T(8,128)(2,1)}, bf16[9,32,192,1,128]{4,2,1,3,0:T(8,128)(2,1)}) fusion(bf16[9,32,192,1,128]{4,2,1,3,0:T(8,128)(2,1)S(1)} %get-tuple-element.30, bf16[34,192,3,130]{3,1,0,2:T(8,128)(2,1)} %all-gather.2.cloned.1.call-done, ...), kind=kLoop, calls=%fused_computation.81 | loop fusion | bytes 9437184
  215.4 8.1 %fusion.46 = (bf16[9,32,192,1,128]{4,2,1,3,0:T(8,128)(2,1)S(1)}, bf16[9,32,192,1,128]{4,2,1,3,0:T(8,128)(2,1)}, bf16[9,32,192,1,128]{4,2,1,3,0:T(8,128)(2,1)}) fusion(bf16[9,32,192,1,128]{4,2,1,3,0:T(8,128)(2,1)S(1)} %get-tuple-element.27, bf16[34,192,3,130]{3,1,0,2:T(8,128)(2,1)} %all-gather.2.cloned.1.call-done, ...), kind=kLoop, calls=%fused_computation.79 | loop fusion | bytes 9437184
  223.5 4.7 fusion.45
  228.2 7.8 %fusion.44 = (bf16[9,32,192,1,128]{4,2,1,3,0:T(8,128)(2,1)S(1)}, bf16[9,32,192,1,128]{4,2,1,3,0:T(8,128)(2,1)}, bf16[9,32,192,1,128]{4,2,1,3,0:T(8,128)(2,1)}) fusion(bf16[9,32,192,1,128]{4,2,1,3,0:T(8,128)(2,1)S(1)} %get-tuple-element.21, bf16[34,192,3,130]{3,1,0,2:T(8,128)(2,1)} %all-gather.2.cloned.1.call-done, ...), kind=kLoop, calls=%fused_computation.75 | loop fusion | bytes 9437184
  236.1 7.9 %fusion.43 = (bf16[9,32,192,1,128]{4,2,1,3,0:T(8,128)(2,1)S(1)}, bf16[9,32,192,1,128]{4,2,1,3,0:T(8,128)(2,1)}, bf16[9,32,192,1,128]{4,2,1,3,0:T(8,128)(2,1)}) fusion(bf16[9,32,192,1,128]{4,2,1,3,0:T(8,128)(2,1)S(1)} %get-tuple-element.18, bf16[34,192,3,130]{3,1,0,2:T(8,128)(2,1)} %all-gather.2.cloned.1.call-done, ...), kind=kLoop, calls=%fused_computation.73 | loop fusion | bytes 9437184
  243.9 4.6 fusion.42
  248.6 8.0 %fusion.41 = (bf16[9,32,192,1,128]{4,2,1,3,0:T(8,128)(2,1)S(1)}, bf16[9,32,192,1,128]{4,2,1,3,0:T(8,128)(2,1)}, bf16[9,32,192,1,128]{4,2,1,3,0:T(8,128)(2,1)}) fusion(bf16[9,32,192,1,128]{4,2,1,3,0:T(8,128)(2,1)S(1)} %get-tuple-element.12, bf16[34,192,3,130]{3,1,0,2:T(8,128)(2,1)} %all-gather.2.cloned.1.call-done, ...), kind=kLoop, calls=%fused_computation.69 | loop fusion | bytes 9437184
  256.6 8.0 %fusion.40 = (bf16[9,32,192,1,128]{4,2,1,3,0:T(8,128)(2,1)S(1)}, bf16[9,32,192,1,128]{4,2,1,3,0:T(8,128)(2,1)}, bf16[9,32,192,1,128]{4,2,1,3,0:T(8,128)(2,1)}) fusion(bf16[9,32,192,1,128]{4,2,1,3,0:T(8,128)(2,1)S(1)} %get-tuple-element.9, bf16[34,192,3,130]{3,1,0,2:T(8,128)(2,1)} %all-gather.2.cloned.1.call-done, ...), kind=kLoop, calls=%fused_computation.67 | loop fusion | bytes 9437184 | tf_op jit(solution)/shard_map/stack | solution.py:61
  264.5 4.0 fusion.59
  268.5 8.9 %fusion.65 = f32[9,24,192]{2,1,0:T(8,128)S(1)} fusion(bf16[9,32,192,1,128]{4,2,1,3,0:T(8,128)(2,1)} %get-tuple-element.7, bf16[32,24,128]{2,0,1:T(8,128)(2,1)S(1)} %convolution_convert_fusion), kind=kOutput, calls=%fused_computation.97 | convolution fusion | flops 339738624 | bytes 14518272 | tf_op jit(solution)/shard_map/forw,kfcrw->koc/dot_general | solution.py:63
  277.6 3.8 fusion.62
  281.3 0.9 maximum_multiply_fusion
  282.3 41.6 %psum.22 = f32[32,128]{1,0:T(8,128)S(1)} all-reduce(f32[32,128]{1,0:T(8,128)S(1)} %get-tuple-element.58), channel_id=1, replica_groups=mesh['rows'=32,'chan'=8] {'chan'}, use_global_device_ids=true, to_apply=%region_4.5 | all-reduce | flops 4096 | bytes 32768 | tf_op jit(solution)/shard_map/psum | solution.py:102
  323.9 1.0 fusion.87
  324.9 270.8 %all-reduce.4.cloned.1.call-done = f32[27,24,192]{2,1,0:T(8,128)} async-done(((f32[27,24,192]{2,1,0:T(8,128)}), f32[27,24,192]{2,1,0:T(8,128)}) %all-reduce.4.cloned.1.call-update) | async-done | bytes 497680 | tf_op jit(solution)/shard_map/psum | solution.py:98
  595.7 2.0 copy.102
  (19 shorter events, 0.4 us)
Async XLA Ops:
  7.2 87.2 %reduce-scatter.2.cloned.1.call-start = ((), (), s32[]{:S(2)}) async-start(), calls=%async_computation.2 | async-start | bytes 3538944 | tf_op jit(solution)/shard_map/reduce_scatter | solution.py:97
  25.6 9.0 %collective-permute-start.1 = (bf16[32,24,1,128]{3,0,1,2:T(8,128)(2,1)S(1)}, bf16[32,24,1,128]{3,0,1,2:T(8,128)(2,1)S(1)}, u32[]{:S(2)}, u32[]{:S(2)}) collective-permute-start(bf16[32,24,1,128]{3,0,1,2:T(8,128)(2,1)S(1)} %bitcast.306), channel_id=1, source_target_pairs={{8,0},{16,8},{24,16},{32,24},{40,32},{48,40},{56,48},{64,56},{72,6... | collective-permute-start | bytes 589832 | tf_op jit(solution)/shard_map/ppermute | solution.py:20
  29.1 9.2 %collective-permute-start = (bf16[32,24,1,128]{3,0,1,2:T(8,128)(2,1)S(1)}, bf16[32,24,1,128]{3,0,1,2:T(8,128)(2,1)S(1)}, u32[]{:S(2)}, u32[]{:S(2)}) collective-permute-start(bf16[32,24,1,128]{3,0,1,2:T(8,128)(2,1)S(1)} %bitcast.307), channel_id=1, source_target_pairs={{0,8},{8,16},{16,24},{24,32},{32,40},{40,48},{48,56},{56,64},{64,7... | collective-permute-start | bytes 589832 | tf_op jit(solution)/shard_map/ppermute | solution.py:17
  40.6 1.0 copy-start.3
  46.2 0.9 copy-start.1
  46.2 48.2 %copy-start.4 = (f32[24]{0:T(128)S(1)}, f32[24]{0:T(128)}, u32[]{:S(2)}) copy-start(f32[24]{0:T(128)} %param.8) | copy-start | bytes 292
  46.2 156.6 %all-gather.2.cloned.1.call-start = ((), (), s32[]{:S(2)}) async-start(), calls=%async_computation.3 | async-start | bytes 11280384 | tf_op jit(solution)/shard_map/all_gather | solution.py:92
  95.7 10.8 %collective-permute-start.3 = (bf16[32,24,1,128]{3,1,0,2:T(8,128)(2,1)S(1)}, bf16[32,24,1,128]{3,1,0,2:T(8,128)(2,1)S(1)}, u32[]{:S(2)}, u32[]{:S(2)}) collective-permute-start(bf16[32,24,1,128]{3,1,0,2:T(8,128)(2,1)S(1)} %get-tuple-element.57), channel_id=1, source_target_pairs={{8,0},{16,8},{24,16},{32,24},{40,32},{48,40},{56,48},{64,56},{72,6... | collective-permute-start | bytes 589832 | tf_op jit(solution)/shard_map/ppermute | solution.py:20
  100.0 11.7 %collective-permute-start.2 = (bf16[32,24,1,128]{3,1,0,2:T(8,128)(2,1)S(1)}, bf16[32,24,1,128]{3,1,0,2:T(8,128)(2,1)S(1)}, u32[]{:S(2)}, u32[]{:S(2)}) collective-permute-start(bf16[32,24,1,128]{3,1,0,2:T(8,128)(2,1)S(1)} %get-tuple-element.57), channel_id=1, source_target_pairs={{0,8},{8,16},{16,24},{24,32},{32,40},{40,48},{48,56},{56,64},{64,7... | collective-permute-start | bytes 589832 | tf_op jit(solution)/shard_map/ppermute | solution.py:17
  113.4 482.3 %all-reduce.4.cloned.1.call-start = ((), (), s32[]{:S(2)}) async-start(), calls=%async_computation.4 | async-start | bytes 1327104 | tf_op jit(solution)/shard_map/psum | solution.py:98
  268.5 9.1 %copy-start = (bf16[9,32,192,1,128]{4,2,1,3,0:T(8,128)(2,1)S(1)}, bf16[9,32,192,1,128]{4,2,1,3,0:T(8,128)(2,1)}, u32[]{:S(2)}) copy-start(bf16[9,32,192,1,128]{4,2,1,3,0:T(8,128)(2,1)} %get-tuple-element.8) | copy-start | bytes 42467332
  281.3 42.6 %copy-start.2 = (f32[32,24,1,128]{3,1,0,2:T(8,128)S(1)}, f32[32,24,1,128]{3,1,0,2:T(8,128)}, u32[]{:S(2)}) copy-start(f32[32,24,1,128]{3,1,0,2:T(8,128)} %reduce-scatter.2.cloned.1.call-done) | copy-start | bytes 1179652
Sparse Core Ops, SparseCore 0:
  46.3 48.0 reduce-scatter.1
  113.5 89.2 all-gather.1
  282.4 313.2 all-reduce.3
where the time goes:
time: 606 us; the launch traced here: 604 us
  waiting for transfers between devices  390 us (64%)
  blocking collectives  91.4 us (15%)
  local copies, waits for them, and re-layouts  68.4 us (11%)
  matrix products  22 us (4%)
  between operations  13.9 us (2%)
  starting transfers between devices  13.2 us (2%)
    psum x1, waiting for transfers between devices, shards(): weight_adjoint = lax.psum(local_grad, 'rows')  271 us
    all_gather x1, waiting for transfers between devices, shards(): lax.all_gather(hidden_pad, 'chan', axis=1, tiled=True)  89.1 us
    unnamed x31, local copies, waits for them, and re-layouts  60.3 us
    psum x1, blocking collectives, shards(): lax.psum(jnp.sum(normed_adjoint * values, axis=1), 'chan')[:, None]  41.6 us
    psum x1, blocking collectives, shards(): squares = lax.psum(jnp.sum(values * values, axis=1), 'chan')  33.2 us
    dot_general x3, matrix products, kernel_grad(): jnp.einsum('forw,kfcrw->koc', adjoint, stacked, preferred_element_type=jn...  16.7 us
    all_to_all x1, blocking collectives, shards(): lax.all_to_all(frame_adjoint, 'rows', split_axis=2, concat_axis=0, tiled=...  16.5 us
    reduce_scatter x1, waiting for transfers between devices, shards(): lax.psum_scatter(partial_sum, 'chan', scatter_dimension=1, tiled=True)  14 us
  transfers between devices with their start and end apart: 7, of which 7 were waited for; matrix products, arithmetic and copies ran while one was open for 0% of the time, Pallas kernels for 0%

commit v1 on v0

v1 whole, which is shorter than its diff:
```python
import jax
import jax.numpy as jnp
from jax import lax
from jax.experimental import pallas as pl
from jax.experimental.pallas import tpu as pltpu
from jax.sharding import PartitionSpec as P

CHANNELS = 192
GROUP = 24
WIDTH = 128
ROWS = 32
CHAN = 8
HALF = 4
TAPS = 27
WINDOW = 80
SLAB = 72
KBLOCK = 224
EPSILON = 1e-06
MESH = pl.DeviceIdType.MESH
VMEM_LIMIT = 56 * 1024 * 1024


def greet(rows_me, chan_me):
    barrier = pltpu.get_barrier_semaphore()

    def rows_step(d, carry):
        pl.semaphore_signal(
            barrier, inc=1, device_id={"rows": lax.rem(rows_me + d, ROWS)}, device_id_type=MESH
        )
        return carry

    def chan_step(d, carry):
        pl.semaphore_signal(
            barrier, inc=1, device_id={"chan": lax.rem(chan_me + d, CHAN)}, device_id_type=MESH
        )
        return carry

    lax.fori_loop(1, ROWS, rows_step, 0)
    lax.fori_loop(1, CHAN, chan_step, 0)
    pl.semaphore_wait(barrier, ROWS - 1 + CHAN - 1)


def send(src, dst, send_sem, recv_sem, device):
    pltpu.make_async_remote_copy(
        src_ref=src,
        dst_ref=dst,
        send_sem=send_sem,
        recv_sem=recv_sem,
        device_id=device,
        device_id_type=MESH,
    ).start()


def drain(ref, sem):
    pltpu.make_async_copy(ref, ref, sem).wait()


def exchange_kernel(
    inverse, win, x, gain, w, adj_out, x_out, gain_out, w_out, recv, ordered, sems, local
):
    r = lax.axis_index("rows")
    c = lax.axis_index("chan")
    h = c // 2
    win_s, win_r, x_s, x_r, g_s, g_r, w_s, w_r, a_s, a_r = [sems.at[i] for i in range(10)]

    own_win = pltpu.make_async_copy(win.at[r], recv.at[r], local.at[0])
    own_win.start()
    greet(r, c)

    def win_step(d, carry):
        target = lax.rem(r + d, ROWS)
        send(win.at[target], recv.at[r], win_s, win_r, {"rows": target})
        return carry

    lax.fori_loop(1, ROWS, win_step, 0)

    def x_step(d, carry):
        target = lax.rem(c + d, CHAN)
        begin = pl.multiple_of((target // 2) * 192, 64)
        send(x.at[pl.ds(begin, 192)], x_out.at[c], x_s, x_r, {"chan": target})
        send(gain, gain_out.at[c], g_s, g_r, {"chan": target})
        return carry

    lax.fori_loop(1, CHAN, x_step, 0)

    def w_step(d, carry):
        target = lax.rem(c + 2 * d, CHAN)
        send(w, w_out.at[h], w_s, w_r, {"chan": target})
        return carry

    lax.fori_loop(1, HALF, w_step, 0)
    begin = pl.multiple_of(h * 192, 64)
    own_x = pltpu.make_async_copy(x.at[pl.ds(begin, 192)], x_out.at[c], local.at[1])
    own_gain = pltpu.make_async_copy(gain, gain_out.at[c], local.at[2])
    own_w = pltpu.make_async_copy(w, w_out.at[h], local.at[3])
    own_x.start()
    own_gain.start()
    own_w.start()

    ordered[pl.ds(32 * SLAB, 2 * SLAB), :] = jnp.zeros((2 * SLAB, WIDTH), jnp.bfloat16)
    own_win.wait()
    drain(recv.at[pl.ds(0, ROWS - 1)], win_r)

    def order_step(p, carry):
        low = recv[inverse[2 * p]].astype(jnp.float32)[:SLAB]
        high = recv[inverse[2 * p + 1]].astype(jnp.float32)[:SLAB]
        both = jnp.concatenate([low, high], axis=0).astype(jnp.bfloat16)
        ordered[pl.ds(pl.multiple_of(p * 2 * SLAB, 2 * SLAB), 2 * SLAB), :] = both
        return carry

    lax.fori_loop(0, ROWS // 2, order_step, 0)

    def a_step(d, carry):
        target = lax.rem(c + 2 * d, CHAN)
        start = pl.multiple_of((target // 2) * (8 * SLAB), 64)
        send(ordered.at[pl.ds(start, 10 * SLAB)], adj_out.at[h], a_s, a_r, {"chan": target})
        return carry

    lax.fori_loop(1, HALF, a_step, 0)
    start = pl.multiple_of(h * (8 * SLAB), 64)
    own_adj = pltpu.make_async_copy(
        ordered.at[pl.ds(start, 10 * SLAB)], adj_out.at[h], local.at[4]
    )
    own_adj.start()
    own_x.wait()
    own_gain.wait()
    own_w.wait()
    own_adj.wait()
    drain(win.at[pl.ds(0, ROWS - 1)], win_s)
    drain(x_out.at[pl.ds(0, CHAN - 1)], x_s)
    drain(gain_out.at[pl.ds(0, CHAN - 1)], g_s)
    drain(w_out.at[pl.ds(0, HALF - 1)], w_s)
    drain(adj_out.at[pl.ds(0, HALF - 1)], a_s)
    drain(x_out.at[pl.ds(0, CHAN - 1)], x_r)
    drain(gain_out.at[pl.ds(0, CHAN - 1)], g_r)
    drain(w_out.at[pl.ds(0, HALF - 1)], w_r)
    drain(adj_out.at[pl.ds(0, HALF - 1)], a_r)


def exchange(inverse, win, x, gain, w):
    anywhere = pl.BlockSpec(memory_space=pl.ANY)
    return pl.pallas_call(
        exchange_kernel,
        out_shape=(
            jax.ShapeDtypeStruct((HALF, 10 * SLAB, WIDTH), jnp.bfloat16),
            jax.ShapeDtypeStruct((CHAN, 8 * GROUP, WIDTH), jnp.bfloat16),
            jax.ShapeDtypeStruct((CHAN, GROUP, WIDTH), jnp.float32),
            jax.ShapeDtypeStruct((HALF, 3 * KBLOCK, CHANNELS), jnp.bfloat16),
        ),
        in_specs=[pl.BlockSpec(memory_space=pltpu.SMEM)] + [anywhere] * 4,
        out_specs=(anywhere,) * 4,
        scratch_shapes=[
            pltpu.VMEM((ROWS, WINDOW, WIDTH), jnp.bfloat16),
            pltpu.VMEM((34 * SLAB, WIDTH), jnp.bfloat16),
            pltpu.SemaphoreType.DMA((10,)),
            pltpu.SemaphoreType.DMA((5,)),
        ],
        compiler_params=pltpu.CompilerParams(
            collective_id=0, has_side_effects=True, vmem_limit_bytes=VMEM_LIMIT
        ),
    )(inverse, win, x, gain, w)


def norm_of(values, gain):
    squares = jnp.sum(values * values, axis=0, keepdims=True)
    scale = lax.rsqrt(squares / CHANNELS + EPSILON)
    return scale, values * scale * gain


def sigmoid(v):
    return 1.0 / (1.0 + jnp.exp(-v))


def compute_kernel(adj, x, gain, w, grad_out, part_out, stack, hidden):
    gains = gain[...]
    for f in range(8):
        values = jnp.concatenate(
            [x[g].astype(jnp.float32)[GROUP * f : GROUP * f + GROUP] for g in range(CHAN)], axis=0
        )
        _, normed = norm_of(values, gains)
        hidden[:, WIDTH * f : WIDTH * (f + 1)] = (normed * sigmoid(normed)).astype(jnp.bfloat16)

    lane = lax.broadcasted_iota(jnp.int32, (10 * SLAB, WIDTH), 1)

    def stack_step(g, carry):
        middle = adj[g].astype(jnp.float32)
        ahead = jnp.where(lane == WIDTH - 1, 0.0, pltpu.roll(middle, WIDTH - 1, 1))
        behind = jnp.where(lane == 0, 0.0, pltpu.roll(middle, 1, 1))
        empty = jnp.zeros((KBLOCK - 3 * SLAB, WIDTH), jnp.float32)
        for col, shifted in enumerate((ahead, middle, behind)):
            for f in range(8):
                slab = jnp.concatenate(
                    [shifted[SLAB * f : SLAB * f + 3 * SLAB], empty], axis=0
                )
                stack[col, g, :, WIDTH * f : WIDTH * (f + 1)] = slab.astype(jnp.bfloat16)
        return carry

    lax.fori_loop(0, HALF, stack_step, 0)

    def grad_step(col, carry):
        sums = [
            lax.dot_general(
                stack[col, g],
                hidden[...],
                (((1,), (1,)), ((), ())),
                preferred_element_type=jnp.float32,
            )
            for g in range(HALF)
        ]
        for a in range(3):
            for b in range(3):
                begin = SLAB * (2 - a) + GROUP * (2 - b)
                piece = jnp.concatenate([s[begin : begin + GROUP] for s in sums], axis=0)
                grad_out[9 * a + 3 * b + col] = piece.astype(jnp.bfloat16)
        return carry

    lax.fori_loop(0, 3, grad_step, 0)

    def part_step(p, carry):
        pixels = pl.ds(pl.multiple_of(p * 256, 256), 256)
        total = jnp.zeros((CHANNELS, 256), jnp.float32)
        for col in range(3):
            for g in range(HALF):
                total = total + lax.dot_general(
                    w[g, KBLOCK * col : KBLOCK * (col + 1), :],
                    stack[col, g, :, pixels],
                    (((0,), (0,)), ((), ())),
                    preferred_element_type=jnp.float32,
                )
        part_out[2 * p] = total[:, :WIDTH]
        part_out[2 * p + 1] = total[:, WIDTH:]
        return carry

    lax.fori_loop(0, 4, part_step, 0)


def compute(adj, x, gain, w):
    return pl.pallas_call(
        compute_kernel,
        out_shape=(
            jax.ShapeDtypeStruct((TAPS, HALF * GROUP, CHANNELS), jnp.bfloat16),
            jax.ShapeDtypeStruct((8, CHANNELS, WIDTH), jnp.float32),
        ),
        scratch_shapes=[
            pltpu.VMEM((3, HALF, KBLOCK, 8 * WIDTH), jnp.bfloat16),
            pltpu.VMEM((CHANNELS, 8 * WIDTH), jnp.bfloat16),
        ],
        compiler_params=pltpu.CompilerParams(vmem_limit_bytes=VMEM_LIMIT),
    )(adj, x, gain, w)


def finish_kernel(
    grad, part, x, gain, x_grad, w_grad, grad_in, part_in, staged, red, red_in, final, sems, local
):
    r = lax.axis_index("rows")
    c = lax.axis_index("chan")
    h = c // 2
    k = lax.rem(c, 2)
    grad_s, grad_r, part_s, part_r, out_s, out_r, red_s, red_r, fin_s, fin_r = [
        sems.at[i] for i in range(10)
    ]
    greet(r, c)

    def grad_send(d, carry):
        target = lax.rem(r + d, ROWS)

        @pl.when(target < TAPS)
        def _():
            send(grad.at[target], grad_in.at[r], grad_s, grad_r, {"rows": target})

        return carry

    part_away = part.at[pl.ds(4 * (1 - k), 4)]
    send(part_away, part_in, part_s, part_r, {"chan": c + 1 - 2 * k})
    lax.fori_loop(1, ROWS, grad_send, 0)

    drain(part_in, part_r)
    gains = gain[...]
    mine = [
        x[g, pl.ds(pl.multiple_of(k * 96, 32), 96), :].astype(jnp.float32) for g in range(CHAN)
    ]
    results = []
    for f in range(4):
        values = jnp.concatenate([m[GROUP * f : GROUP * f + GROUP] for m in mine], axis=0)
        scale, normed = norm_of(values, gains)
        s = sigmoid(normed)
        adjoint = part[4 * k + f] + part_in[f]
        normed_adjoint = adjoint * s * (1.0 + normed * (1.0 - s)) * gains
        projection = jnp.sum(normed_adjoint * values, axis=0, keepdims=True)
        results.append(
            scale * normed_adjoint - values * (scale * scale * scale * projection / CHANNELS)
        )
    for g in range(CHAN):
        rows = jnp.concatenate([y[GROUP * g : GROUP * g + GROUP] for y in results], axis=0)
        staged[g] = rows.astype(jnp.bfloat16)

    here = pl.ds(pl.multiple_of(c * 96, 32), 96)

    def out_step(d, carry):
        target = lax.rem(c + d, CHAN)
        send(staged.at[target], x_grad.at[here], out_s, out_r, {"chan": target})
        return carry

    lax.fori_loop(1, CHAN, out_step, 0)
    own_out = pltpu.make_async_copy(staged.at[c], x_grad.at[here], local.at[0])
    own_out.start()

    @pl.when(r < TAPS)
    def _():
        own_grad = pltpu.make_async_copy(grad.at[r], grad_in.at[r], local.at[1])
        own_grad.start()
        own_grad.wait()
        drain(grad_in.at[pl.ds(0, ROWS - 1)], grad_r)

        def add_step(i, total):
            return total + grad_in[i].astype(jnp.float32)

        total = lax.fori_loop(
            0, ROWS, add_step, jnp.zeros((HALF * GROUP, CHANNELS), jnp.float32)
        )
        for g in range(HALF):
            red[g] = total[GROUP * g : GROUP * (g + 1)]

        def red_step(d, carry):
            target = lax.rem(c + 2 * d, CHAN)
            send(red.at[target // 2], red_in.at[h], red_s, red_r, {"chan": target})
            return carry

        lax.fori_loop(1, HALF, red_step, 0)
        own_red = pltpu.make_async_copy(red.at[h], red_in.at[h], local.at[2])
        own_red.start()
        own_red.wait()
        drain(red_in.at[pl.ds(0, HALF - 1)], red_r)
        whole = red_in[0] + red_in[1] + red_in[2] + red_in[3]
        final[...] = whole * float(ROWS * ROWS * WIDTH) ** (-0.5)

        def final_step(d, carry):
            target = lax.rem(r + d, ROWS)
            send(final, w_grad.at[r], fin_s, fin_r, {"rows": target})
            return carry

        lax.fori_loop(1, ROWS, final_step, 0)
        own_final = pltpu.make_async_copy(final, w_grad.at[r], local.at[3])
        own_final.start()
        own_final.wait()
        drain(grad.at[pl.ds(0, TAPS - 1)], grad_s)
        drain(red.at[pl.ds(0, HALF - 1)], red_s)
        drain(w_grad.at[pl.ds(0, TAPS - 1)], fin_r)

        def sent_step(d, carry):
            drain(final, fin_s)
            return carry

        lax.fori_loop(1, ROWS, sent_step, 0)

    @pl.when(r >= TAPS)
    def _():
        drain(grad.at[pl.ds(0, TAPS)], grad_s)
        drain(w_grad.at[pl.ds(0, TAPS)], fin_r)

    drain(part_in, part_s)
    own_out.wait()
    drain(staged.at[pl.ds(0, CHAN - 1)], out_s)
    drain(x_grad.at[pl.ds(0, (CHAN - 1) * 96)], out_r)


def finish(grad, part, x, gain):
    anywhere = pl.BlockSpec(memory_space=pl.ANY)
    vmem = pl.BlockSpec(memory_space=pltpu.VMEM)
    return pl.pallas_call(
        finish_kernel,
        out_shape=(
            jax.ShapeDtypeStruct((ROWS * GROUP, WIDTH), jnp.bfloat16),
            jax.ShapeDtypeStruct((TAPS, GROUP, CHANNELS), jnp.float32),
        ),
        in_specs=[vmem] * 4,
        out_specs=(anywhere, anywhere),
        scratch_shapes=[
            pltpu.VMEM((ROWS, HALF * GROUP, CHANNELS), jnp.bfloat16),
            pltpu.VMEM((4, CHANNELS, WIDTH), jnp.float32),
            pltpu.VMEM((CHAN, 4 * GROUP, WIDTH), jnp.bfloat16),
            pltpu.VMEM((HALF, GROUP, CHANNELS), jnp.float32),
            pltpu.VMEM((HALF, GROUP, CHANNELS), jnp.float32),
            pltpu.VMEM((GROUP, CHANNELS), jnp.float32),
            pltpu.SemaphoreType.DMA((10,)),
            pltpu.SemaphoreType.DMA((4,)),
        ],
        compiler_params=pltpu.CompilerParams(
            collective_id=1, has_side_effects=True, vmem_limit_bytes=VMEM_LIMIT
        ),
    )(grad, part, x, gain)


def shards(frame_adjoint, frame_slot, inputs, gain, weight):
    slots = jnp.arange(ROWS, dtype=jnp.int32)
    inverse = jnp.sum(jnp.where(frame_slot[None, :] == slots[:, None], slots[None, :], 0), axis=1)
    by_row = jnp.pad(jnp.transpose(frame_adjoint[0], (1, 0, 2)), ((1, 1), (0, 0), (0, 0)))
    windows = jnp.concatenate(
        [by_row[:ROWS], by_row[1 : ROWS + 1], by_row[2:], jnp.zeros((ROWS, 8, WIDTH), jnp.bfloat16)],
        axis=1,
    )
    taps = weight.reshape(3, 3, 3, GROUP, CHANNELS)[::-1, ::-1]
    taps = jnp.transpose(taps, (2, 0, 1, 3, 4)).reshape(3, 3 * SLAB, CHANNELS)
    taps = jnp.pad(taps, ((0, 0), (0, KBLOCK - 3 * SLAB), (0, 0))).reshape(3 * KBLOCK, CHANNELS)
    values = inputs.reshape(ROWS * GROUP, WIDTH)
    gains = jnp.broadcast_to(gain[:, None], (GROUP, WIDTH))
    adj, x, gain_all, w = exchange(inverse, windows, values, gains, taps)
    gain_all = gain_all.reshape(CHANNELS, WIDTH)
    grad, part = compute(adj, x, gain_all, w)
    input_adjoint, weight_adjoint = finish(grad, part, x, gain_all)
    return input_adjoint.reshape(ROWS, GROUP, 1, WIDTH), weight_adjoint


def solution(mesh):
    in_specs = (
        P("rows", "chan", None, None),
        P(),
        P(None, "chan", "rows", None),
        P("chan"),
        P(None, "chan", None),
    )
    out_specs = (P(None, "chan", "rows", None), P(None, "chan", None))
    return jax.shard_map(shards, mesh=mesh, in_specs=in_specs, out_specs=out_specs, check_vma=False)
```

time: 606 us -> 141 us (0.23)
  waiting for transfers between devices: 390 us -> 0 us
  Pallas kernels: 0 us -> 130 us
  blocking collectives: 91.4 us -> 0 us
  local copies, waits for them, and re-layouts: 68.4 us -> 7.87 us
  matrix products: 22 us -> 0 us
  between operations: 13.9 us -> 0.67 us
  starting transfers between devices: 13.2 us -> 0 us
    psum x1 -> x0, waiting for transfers between devices: 271 us -> none  [shards(): weight_adjoint = lax.psum(local_grad, 'rows')]
    pallas_call x0 -> x3, Pallas kernels: none -> 130 us  [the longest x1 74.9 us: exchange(): pl.pallas_call(exchange_kernel, out_shape=(jax.ShapeDtypeStruct((HALF, 10...]
    all_gather x1 -> x0, waiting for transfers between devices: 89.1 us -> none  [shards(): lax.all_gather(hidden_pad, 'chan', axis=1, tiled=True)]
    psum x2 -> x0, blocking collectives: 74.9 us -> none  [the longest x1 41.6 us: shards(): lax.psum(jnp.sum(normed_adjoint * values, axis=1), 'chan')[:, None]]
    unnamed x31 -> x3, local copies, waits for them, and re-layouts: 60.3 us -> 4.6 us
    dot_general x7 -> x0, matrix products: 22 us -> none  [the longest x3 16.7 us: kernel_grad(): jnp.einsum('forw,kfcrw->koc', adjoint, stacked, preferred_element_type=jn...]
    all_to_all x1 -> x0, blocking collectives: 16.5 us -> none  [shards(): lax.all_to_all(frame_adjoint, 'rows', split_axis=2, concat_axis=0, tiled=...]
    ppermute x4 -> x0, waiting for transfers between devices: 15.8 us -> none  [the longest x2 8.87 us: extended(): lax.ppermute(lax.slice_in_dim(block, block.shape[dim] - width, None, axis...]
  transfers between devices with their start and end apart: 7 -> 0, of which waited for: 7 -> 0; matrix products, arithmetic and copies ran while one was open for 0% -> 0% of each run, Pallas kernels for 0% -> 0%
where the time goes in v1:
time: 141 us; the launch traced here: 140 us
  Pallas kernels  130 us (92%)
  local copies, waits for them, and re-layouts  7.87 us (6%)
  other arithmetic  2.28 us (2%)
    pallas_call x1, Pallas kernels, exchange(): pl.pallas_call(exchange_kernel, out_shape=(jax.ShapeDtypeStruct((HALF, 10...  74.9 us
    pallas_call x1, Pallas kernels, finish(): pl.pallas_call(finish_kernel, out_shape=(jax.ShapeDtypeStruct((ROWS * GRO...  46.1 us
    pallas_call x1, Pallas kernels, compute(): pl.pallas_call(compute_kernel, out_shape=(jax.ShapeDtypeStruct((TAPS, HAL...  8.44 us
    unnamed x3, local copies, waits for them, and re-layouts  4.6 us

profile of v1, /device:TPU:8, one launch (start us, length us, event | category | flops | bytes accessed | tf_op | source)
XLA Modules:
  0.0 140.3 jit_solution(13007354628079572703)
XLA Ops:
  0.6 1.3 select_reduce_fusion.inverse
  1.9 0.1 pad.13.clone
  2.0 1.3 broadcast_in_dim.27.gain
  3.3 1.0 copy.14
  4.3 1.0 reverse_bitcast_fusion
  5.3 0.8 pad.9
  6.1 0.1 pad_slice_fusion.1
  6.2 1.0 maximum_maximum_fusion.win
  7.2 74.9 %shard_map.68 = (bf16[4,720,128]{2,1,0:T(8,128)(2,1)}, bf16[8,192,128]{2,1,0:T(8,128)(2,1)}, f32[8,24,128]{2,1,0:T(8,128)}, bf16[4,672,192]{2,1,0:T(8,128)(2,1)}) custom-call(s32[32]{0:T(128)} %select_reduce_fusion.inverse, bf16[32,80,128]{2,1,0:T(8,128)(2,1)} %maximum_maximum_fusion.win, bf16[768,128]{1,0:T(8,128)(2,1)} %bitcast.23, ...), custom_call_target="tpu_custom_call" | custom-call | tf_op jit(solution)/shard_map/pallas_call | solution.py:142
  82.1 8.4 %shard_map.69 = (bf16[27,96,192]{2,1,0:T(8,128)(2,1)}, f32[8,192,128]{2,1,0:T(8,128)}) custom-call(bf16[4,720,128]{2,1,0:T(8,128)(2,1)} %get-tuple-element.10.adj, bf16[8,192,128]{2,1,0:T(8,128)(2,1)} %get-tuple-element.11.x, f32[192,128]{1,0:T(8,128)} %bitcast.19, bf16[4,672,192]{2,1,0:T(8,128)(2,1)} %get-tuple-element.13.w), custom_call_target="tpu_custom_call" | custom-call | tf_op jit(solution)/shard_map/pallas_call | solution.py:238
  90.6 46.1 %shard_map.70 = (bf16[768,128]{1,0:T(8,128)(2,1)}, f32[27,24,192]{2,1,0:T(8,128)}) custom-call(bf16[27,96,192]{2,1,0:T(8,128)(2,1)} %get-tuple-element.14.grad, f32[8,192,128]{2,1,0:T(8,128)} %get-tuple-element.15.part, bf16[8,192,128]{2,1,0:T(8,128)(2,1)} %get-tuple-element.11.x, f32[192,128]{1,0:T(8,128)} %bitcast.20), custom_call_target="tpu_custom_call" | custom-call | tf_op jit(solution)/shard_map/pallas_call | solution.py:370
  136.7 1.6 %copy.17 = bf16[32,24,1,128]{3,1,2,0:T(8,128)(2,1)} copy(bf16[32,24,1,128]{3,1,2,0:T(8,128)(2,1)} %bitcast.22) | data formatting | bytes 393216
  138.4 2.0 %copy.18 = f32[27,24,192]{2,1,0:T(8,128)} copy(f32[27,24,192]{2,1,0:T(8,128)} %get-tuple-element.27) | data formatting | bytes 995328
  (2 shorter events, 0.0 us)

commit v2 on v0

v2 whole, which is shorter than its diff:
```python
import jax
import jax.numpy as jnp
from jax import lax
from jax.experimental import pallas as pl
from jax.experimental.pallas import tpu as pltpu
from jax.sharding import PartitionSpec as P

CHANNELS = 192
GROUP = 24
WIDTH = 128
ROWS = 32
CHAN = 8
HALF = 4
RING = 4
TAPS = 27
WINDOW = 80
SLAB = 72
KBLOCK = 224
PACK = 1024
LOW = 3 * KBLOCK
PIECE = PACK // ROWS
SLICE = PACK // 8
EPSILON = 1e-06
MESH = pl.DeviceIdType.MESH
VMEM_LIMIT = 56 * 1024 * 1024


def greet(rows_me, chan_me):
    barrier = pltpu.get_barrier_semaphore()

    def rows_step(d, carry):
        pl.semaphore_signal(
            barrier, inc=1, device_id={"rows": lax.rem(rows_me + d, ROWS)}, device_id_type=MESH
        )
        return carry

    def chan_step(d, carry):
        pl.semaphore_signal(
            barrier, inc=1, device_id={"chan": lax.rem(chan_me + d, CHAN)}, device_id_type=MESH
        )
        return carry

    lax.fori_loop(1, ROWS, rows_step, 0)
    lax.fori_loop(1, CHAN, chan_step, 0)
    pl.semaphore_wait(barrier, ROWS - 1 + CHAN - 1)


def send(src, dst, send_sem, recv_sem, device):
    pltpu.make_async_remote_copy(
        src_ref=src,
        dst_ref=dst,
        send_sem=send_sem,
        recv_sem=recv_sem,
        device_id=device,
        device_id_type=MESH,
    ).start()


def drain(ref, sem):
    pltpu.make_async_copy(ref, ref, sem).wait()


def loop(low, high, step):
    def body(i, carry):
        step(i)
        return carry

    lax.fori_loop(low, high, body, 0)


def norm_of(values, gain):
    squares = jnp.sum(values * values, axis=0, keepdims=True)
    scale = lax.rsqrt(squares / CHANNELS + EPSILON)
    return scale, values * scale * gain


def sigmoid(v):
    return 1.0 / (1.0 + jnp.exp(-v))


def pair_lanes(low):
    return jnp.concatenate([low[: KBLOCK // 2], low[KBLOCK // 2 :]], axis=1)


def kernel(
    slot,
    gain,
    frames,
    x,
    w,
    x_grad,
    w_grad,
    wide,
    inverse,
    win,
    recv,
    ordered,
    adj,
    x_all,
    gain_all,
    w_all,
    stack,
    hidden,
    part,
    part_in,
    grad,
    grad_in,
    staged,
    red,
    red_in,
    final,
    win_s,
    win_r,
    x_s,
    x_r,
    gain_s,
    gain_r,
    core_s,
    core_r,
    w_s,
    w_r,
    w2_s,
    w2_r,
    a_s,
    a_r,
    grad_s,
    grad_r,
    part_s,
    part_r,
    out_s,
    out_r,
    red_s,
    red_r,
    fin_s,
    fin_r,
    local,
):
    r = lax.axis_index("rows")
    c = lax.axis_index("chan")
    h = c // 2
    k = lax.rem(c, 2)
    chip_x = r // 8
    chip_y = lax.rem(r, 8) // 2
    other = {"chan": c + 1 - 2 * k}

    wide[...] = frames[...].astype(jnp.float32)

    def win_build(i):
        after = wide[pl.ds(jnp.minimum(i + 1, ROWS - 1), GROUP, stride=ROWS), :]
        here = wide[pl.ds(i, GROUP, stride=ROWS), :]
        before = wide[pl.ds(jnp.maximum(i - 1, 0), GROUP, stride=ROWS), :]
        after = jnp.where(i == ROWS - 1, 0.0, after)
        before = jnp.where(i == 0, 0.0, before)
        empty = jnp.zeros((WINDOW - SLAB, WIDTH), jnp.float32)
        win[i] = jnp.concatenate([after, here, before, empty], axis=0).astype(jnp.bfloat16)

    loop(0, ROWS, win_build)
    recv[r] = win[r]
    x_all[k, 0] = x[pl.ds(pl.multiple_of(h * 192, 64), 192), :]
    gain_all[k, 0] = jnp.concatenate(
        [jnp.full((1, WIDTH), gain[j], jnp.float32) for j in range(GROUP)], axis=0
    )
    for col in range(3):
        rows = [w[9 * a + 3 * b + col].astype(jnp.float32) for a in range(3) for b in range(3)]
        rows = jnp.concatenate(
            rows + [jnp.zeros((KBLOCK - 3 * SLAB, CHANNELS), jnp.float32)], axis=0
        )
        w_all[0, KBLOCK * col : KBLOCK * (col + 1), :] = rows[:, :WIDTH].astype(jnp.bfloat16)
        begin = LOW + KBLOCK // 2 * col
        w_all[0, begin : begin + KBLOCK // 2, :] = pair_lanes(rows[:, WIDTH:]).astype(jnp.bfloat16)
    w_all[0, PACK - 16 :, :] = jnp.zeros((16, WIDTH), jnp.bfloat16)
    ordered[pl.ds(32 * SLAB, 2 * SLAB), :] = jnp.zeros((2 * SLAB, WIDTH), jnp.bfloat16)

    greet(r, c)

    def win_send(d):
        target = lax.rem(r + d, ROWS)
        send(win.at[target], recv.at[r], win_s, win_r, {"rows": target})

    along_x = pl.ds(pl.multiple_of(SLICE * chip_x, SLICE), SLICE)
    along_y = pl.ds(pl.multiple_of(SLICE * (RING + chip_y), SLICE), SLICE)

    def x_send(d):
        target = lax.rem(c + 2 * d, CHAN)
        begin = pl.multiple_of((target // 2) * 192, 64)
        send(x.at[pl.ds(begin, 192)], x_all.at[k, HALF - d], x_s, x_r, {"chan": target})
        send(gain_all.at[k, 0], gain_all.at[k, HALF - d], gain_s, gain_r, {"chan": target})

    def w_send(d):
        target = lax.rem(c + 2 * d, CHAN)
        for rows in (along_x, along_y):
            send(w_all.at[0, rows], w_all.at[HALF - d, rows], w_s, w_r, {"chan": target})

    loop(1, HALF, x_send)
    loop(1, ROWS, win_send)
    loop(1, HALF, w_send)

    def invert(t):
        place = jnp.int32(0)
        for j in range(ROWS):
            place = jnp.where(slot[j] == t, j, place)
        inverse[t] = place

    loop(0, ROWS, invert)

    drain(x_all.at[k, pl.ds(1, HALF - 1)], x_r)
    drain(gain_all.at[k, pl.ds(1, HALF - 1)], gain_r)
    send(x_all.at[k], x_all.at[k], core_s.at[0], core_r.at[0], other)
    send(gain_all.at[k], gain_all.at[k], core_s.at[1], core_r.at[1], other)

    drain(recv.at[pl.ds(0, ROWS - 1)], win_r)

    def order_step(p):
        low = recv[inverse[2 * p]].astype(jnp.float32)[:SLAB]
        high = recv[inverse[2 * p + 1]].astype(jnp.float32)[:SLAB]
        both = jnp.concatenate([low, high], axis=0).astype(jnp.bfloat16)
        ordered[pl.ds(pl.multiple_of(p * 2 * SLAB, 2 * SLAB), 2 * SLAB), :] = both

    loop(0, ROWS // 2, order_step)

    def a_send(d):
        target = lax.rem(c + 2 * d, CHAN)
        start = pl.multiple_of((target // 2) * (8 * SLAB), 64)
        send(
            ordered.at[pl.ds(start, 10 * SLAB)],
            adj.at[HALF - d],
            a_s,
            a_r.at[HALF - d],
            {"chan": target},
        )

    for d in (1, 3, 2):
        a_send(d)
    adj[0] = ordered[pl.ds(pl.multiple_of(h * (8 * SLAB), 64), 10 * SLAB), :]

    drain(w_all.at[pl.ds(1, HALF - 1), pl.ds(0, 2 * SLICE)], w_r)

    def w_spread(d):
        to_x = lax.rem(chip_x + d, RING) * 8 + lax.rem(r, 8)
        to_y = chip_x * 8 + lax.rem(lax.rem(r, 8) + 2 * d, 8)
        for rows, target in ((along_x, to_x), (along_y, to_y)):
            block = w_all.at[pl.ds(1, HALF - 1), rows]
            send(block, block, w2_s, w2_r, {"rows": target})

    loop(1, RING, w_spread)

    drain(x_all.at[1 - k], core_r.at[0])
    drain(gain_all.at[1 - k], core_r.at[1])

    def block_of(channel_group):
        return channel_group % 2, lax.rem(channel_group // 2 - h + HALF, HALF)

    gains = jnp.concatenate([gain_all[block_of(g)] for g in range(CHAN)], axis=0)
    for f in range(8):
        values = jnp.concatenate(
            [
                x_all[block_of(g)].astype(jnp.float32)[GROUP * f : GROUP * f + GROUP]
                for g in range(CHAN)
            ],
            axis=0,
        )
        _, normed = norm_of(values, gains)
        hidden[:, WIDTH * f : WIDTH * (f + 1)] = (normed * sigmoid(normed)).astype(jnp.bfloat16)

    part[...] = jnp.zeros((8, CHANNELS, WIDTH), jnp.float32)
    lane = lax.broadcasted_iota(jnp.int32, (10 * SLAB, WIDTH), 1)

    def block_step(d):
        middle = adj[d].astype(jnp.float32)
        ahead = jnp.where(lane == WIDTH - 1, 0.0, pltpu.roll(middle, WIDTH - 1, 1))
        behind = jnp.where(lane == 0, 0.0, pltpu.roll(middle, 1, 1))
        empty = jnp.zeros((KBLOCK - 3 * SLAB, WIDTH), jnp.float32)
        for col, shifted in enumerate((ahead, middle, behind)):
            for f in range(8):
                slab = jnp.concatenate(
                    [shifted[SLAB * (f + 2 - a) : SLAB * (f + 3 - a)] for a in range(3)] + [empty],
                    axis=0,
                )
                stack[col, :, WIDTH * f : WIDTH * (f + 1)] = slab.astype(jnp.bfloat16)

        def grad_step(col):
            sums = lax.dot_general(
                stack[col],
                hidden[...],
                (((1,), (1,)), ((), ())),
                preferred_element_type=jnp.float32,
            )
            top = pl.ds(pl.multiple_of(KBLOCK * col, 32), KBLOCK)
            grad[d, top, :] = sums[:, :WIDTH].astype(jnp.bfloat16)
            bottom = pl.ds(pl.multiple_of(LOW + KBLOCK // 2 * col, 16), KBLOCK // 2)
            grad[d, bottom, :] = pair_lanes(sums[:, WIDTH:]).astype(jnp.bfloat16)

        loop(0, 3, grad_step)
        grad[d, PACK - 16 :, :] = jnp.zeros((16, WIDTH), jnp.bfloat16)
        grad_in[d, r] = grad[d, pl.ds(pl.multiple_of(r * PIECE, PIECE), PIECE), :]

        def grad_send(e):
            target = lax.rem(r + e, ROWS)
            rows = pl.ds(pl.multiple_of(target * PIECE, PIECE), PIECE)
            send(grad.at[d, rows], grad_in.at[d, r], grad_s, grad_r, {"rows": target})

        loop(1, ROWS, grad_send)

    def part_step(d):
        top = []
        bottom = []
        for col in range(3):
            top.append(w_all[d, KBLOCK * col : KBLOCK * (col + 1), :])
            begin = LOW + KBLOCK // 2 * col
            low = w_all[d, begin : begin + KBLOCK // 2, :].astype(jnp.float32)
            both = jnp.concatenate([low, pltpu.roll(low, 64, 1)], axis=0)
            bottom.append(both[:, :64].astype(jnp.bfloat16))

        def pixels_step(p):
            pixels = pl.ds(pl.multiple_of(p * 256, 256), 256)

            def product(weights):
                total = None
                for col in range(3):
                    term = lax.dot_general(
                        weights[col],
                        stack[col, :, pixels],
                        (((0,), (0,)), ((), ())),
                        preferred_element_type=jnp.float32,
                    )
                    total = term if total is None else total + term
                return total

            high = product(top)
            rest = product(bottom)
            for i in range(2):
                lanes = slice(WIDTH * i, WIDTH * (i + 1))
                part[2 * p + i, :WIDTH, :] += high[:, lanes]
                part[2 * p + i, WIDTH:, :] += rest[:, lanes]

        loop(0, 4, pixels_step)

    block_step(0)
    part_step(0)
    drain(w_all.at[pl.ds(1, HALF - 1), pl.ds(0, 6 * SLICE)], w2_r)
    for d in (1, 3, 2):
        drain(adj.at[d], a_r.at[d])
        block_step(d)
        part_step(d)

    send(part.at[pl.ds(4 * (1 - k), 4)], part_in, part_s, part_r, other)
    mine = [
        x_all[block_of(g) + (pl.ds(pl.multiple_of(k * 96, 32), 96),)].astype(jnp.float32)
        for g in range(CHAN)
    ]
    drain(part_in, part_r)
    results = []
    for f in range(4):
        values = jnp.concatenate([m[GROUP * f : GROUP * f + GROUP] for m in mine], axis=0)
        scale, normed = norm_of(values, gains)
        s = sigmoid(normed)
        adjoint = part[4 * k + f] + part_in[f]
        normed_adjoint = adjoint * s * (1.0 + normed * (1.0 - s)) * gains
        projection = jnp.sum(normed_adjoint * values, axis=0, keepdims=True)
        results.append(
            scale * normed_adjoint - values * (scale * scale * scale * projection / CHANNELS)
        )
    for g in range(CHAN):
        rows = jnp.concatenate([y[GROUP * g : GROUP * g + GROUP] for y in results], axis=0)
        staged[g] = rows.astype(jnp.bfloat16)

    mine_out = pl.ds(pl.multiple_of(c * 96, 32), 96)

    def out_send(d):
        target = lax.rem(c + d, CHAN)
        send(staged.at[target], x_grad.at[mine_out], out_s, out_r, {"chan": target})

    loop(1, CHAN, out_send)
    own_out = pltpu.make_async_copy(staged.at[c], x_grad.at[mine_out], local.at[0])
    own_out.start()

    drain(grad_in.at[:, pl.ds(0, ROWS - 1)], grad_r)
    for d in range(HALF):

        def add_step(i, total):
            return total + grad_in[d, i].astype(jnp.float32)

        red[d] = lax.fori_loop(0, ROWS, add_step, jnp.zeros((PIECE, WIDTH), jnp.float32))
    red_in[0] = red[0]

    def red_send(d):
        send(red.at[d], red_in.at[HALF - d], red_s, red_r, {"chan": lax.rem(c + 2 * d, CHAN)})

    loop(1, HALF, red_send)
    drain(red_in.at[pl.ds(1, HALF - 1)], red_r)
    whole = red_in[0] + red_in[1] + red_in[2] + red_in[3]
    final[...] = whole * float(ROWS * ROWS * WIDTH) ** (-0.5)

    def final_send(d):
        send(final, w_grad.at[r], fin_s, fin_r, {"rows": lax.rem(r + d, ROWS)})

    loop(1, ROWS, final_send)
    own_final = pltpu.make_async_copy(final, w_grad.at[r], local.at[1])
    own_final.start()

    drain(win.at[pl.ds(0, ROWS - 1)], win_s)
    drain(x_all.at[k, pl.ds(1, HALF - 1)], x_s)
    drain(gain_all.at[k, pl.ds(1, HALF - 1)], gain_s)
    drain(x_all.at[k], core_s.at[0])
    drain(gain_all.at[k], core_s.at[1])
    drain(w_all.at[pl.ds(1, HALF - 1), pl.ds(0, 2 * SLICE)], w_s)
    drain(w_all.at[pl.ds(1, HALF - 1), pl.ds(0, 6 * SLICE)], w2_s)
    drain(adj.at[pl.ds(1, HALF - 1)], a_s)
    drain(grad_in.at[:, pl.ds(0, ROWS - 1)], grad_s)
    drain(part_in, part_s)
    drain(staged.at[pl.ds(0, CHAN - 1)], out_s)
    drain(red.at[pl.ds(1, HALF - 1)], red_s)
    drain(w_grad.at[pl.ds(0, ROWS - 1)], fin_s)
    own_out.wait()
    own_final.wait()
    drain(x_grad.at[pl.ds(0, (CHAN - 1) * 96)], out_r)
    drain(w_grad.at[pl.ds(0, ROWS - 1)], fin_r)


def backward(slot, gain, frames, x, w):
    anywhere = pl.BlockSpec(memory_space=pl.ANY)
    scalars = pl.BlockSpec(memory_space=pltpu.SMEM)
    vmem = pl.BlockSpec(memory_space=pltpu.VMEM)
    bf16, f32 = jnp.bfloat16, jnp.float32
    one = pltpu.SemaphoreType.DMA
    many = lambda n: pltpu.SemaphoreType.DMA((n,))
    return pl.pallas_call(
        kernel,
        out_shape=(
            jax.ShapeDtypeStruct((ROWS * GROUP, WIDTH), bf16),
            jax.ShapeDtypeStruct((ROWS, PIECE, WIDTH), f32),
        ),
        in_specs=[scalars, scalars, vmem, vmem, vmem],
        out_specs=(anywhere, anywhere),
        scratch_shapes=[
            pltpu.VMEM((GROUP * ROWS, WIDTH), f32),
            pltpu.SMEM((ROWS,), jnp.int32),
            pltpu.VMEM((ROWS, WINDOW, WIDTH), bf16),
            pltpu.VMEM((ROWS, WINDOW, WIDTH), bf16),
            pltpu.VMEM((34 * SLAB, WIDTH), bf16),
            pltpu.VMEM((HALF, 10 * SLAB, WIDTH), bf16),
            pltpu.VMEM((2, HALF, 8 * GROUP, WIDTH), bf16),
            pltpu.VMEM((2, HALF, GROUP, WIDTH), f32),
            pltpu.VMEM((HALF, PACK, WIDTH), bf16),
            pltpu.VMEM((3, KBLOCK, 8 * WIDTH), bf16),
            pltpu.VMEM((CHANNELS, 8 * WIDTH), bf16),
            pltpu.VMEM((8, CHANNELS, WIDTH), f32),
            pltpu.VMEM((4, CHANNELS, WIDTH), f32),
            pltpu.VMEM((HALF, PACK, WIDTH), bf16),
            pltpu.VMEM((HALF, ROWS, PIECE, WIDTH), bf16),
            pltpu.VMEM((CHAN, 4 * GROUP, WIDTH), bf16),
            pltpu.VMEM((HALF, PIECE, WIDTH), f32),
            pltpu.VMEM((HALF, PIECE, WIDTH), f32),
            pltpu.VMEM((PIECE, WIDTH), f32),
            one, one, one, one, one, one,
            many(2), many(2),
            one, one, one, one,
            one, many(HALF),
            one, one, one, one, one, one, one, one, one, one,
            many(2),
        ],
        compiler_params=pltpu.CompilerParams(
            collective_id=0, has_side_effects=True, vmem_limit_bytes=VMEM_LIMIT
        ),
    )(slot, gain, frames, x, w)


def unpack_kernel(x_in, w_in, x_out, w_out):
    x_out[...] = x_in[...]
    for col in range(3):
        low = w_in[LOW + KBLOCK // 2 * col : LOW + KBLOCK // 2 * (col + 1), :]
        low = jnp.concatenate([low, pltpu.roll(low, 64, 1)], axis=0)
        for a in range(3):
            for b in range(3):
                begin = SLAB * a + GROUP * b
                top = w_in[KBLOCK * col + begin : KBLOCK * col + begin + GROUP, :]
                w_out[9 * a + 3 * b + col, :, :WIDTH] = top
                w_out[9 * a + 3 * b + col, :, WIDTH:] = low[begin : begin + GROUP, :64]


def unpack(x, w):
    return pl.pallas_call(
        unpack_kernel,
        out_shape=(
            jax.ShapeDtypeStruct((ROWS * GROUP, WIDTH), jnp.bfloat16),
            jax.ShapeDtypeStruct((TAPS, GROUP, CHANNELS), jnp.float32),
        ),
        compiler_params=pltpu.CompilerParams(vmem_limit_bytes=16 * 1024 * 1024),
    )(x, w)


def shards(frame_adjoint, frame_slot, inputs, gain, weight):
    frames = frame_adjoint.reshape(GROUP * ROWS, WIDTH)
    values = inputs.reshape(ROWS * GROUP, WIDTH)
    x_grad, w_grad = backward(frame_slot, gain, frames, values, weight)
    input_adjoint, weight_adjoint = unpack(x_grad, w_grad.reshape(PACK, WIDTH))
    return input_adjoint.reshape(ROWS, GROUP, 1, WIDTH), weight_adjoint


def solution(mesh):
    in_specs = (
        P("rows", "chan", None, None),
        P(),
        P(None, "chan", "rows", None),
        P("chan"),
        P(None, "chan", None),
    )
    out_specs = (P(None, "chan", "rows", None), P(None, "chan", None))
    return jax.shard_map(shards, mesh=mesh, in_specs=in_specs, out_specs=out_specs, check_vma=False)
```

time: 606 us -> 81 us (0.13)
  waiting for transfers between devices: 390 us -> 0 us
  blocking collectives: 91.4 us -> 0 us
  Pallas kernels: 0 us -> 78.2 us
  local copies, waits for them, and re-layouts: 68.4 us -> 1.96 us
  matrix products: 22 us -> 0 us
  between operations: 13.9 us -> 0.65 us
  starting transfers between devices: 13.2 us -> 0 us
    psum x1 -> x0, waiting for transfers between devices: 271 us -> none  [shards(): weight_adjoint = lax.psum(local_grad, 'rows')]
    all_gather x1 -> x0, waiting for transfers between devices: 89.1 us -> none  [shards(): lax.all_gather(hidden_pad, 'chan', axis=1, tiled=True)]
    pallas_call x0 -> x2, Pallas kernels: none -> 78.2 us  [the longest x1 77.3 us: backward(): pl.pallas_call(kernel, out_shape=(jax.ShapeDtypeStruct((ROWS * GROUP, WID...]
    psum x2 -> x0, blocking collectives: 74.9 us -> none  [the longest x1 41.6 us: shards(): lax.psum(jnp.sum(normed_adjoint * values, axis=1), 'chan')[:, None]]
    unnamed x31 -> x4, local copies, waits for them, and re-layouts: 60.3 us -> 1.96 us
    dot_general x7 -> x0, matrix products: 22 us -> none  [the longest x3 16.7 us: kernel_grad(): jnp.einsum('forw,kfcrw->koc', adjoint, stacked, preferred_element_type=jn...]
    all_to_all x1 -> x0, blocking collectives: 16.5 us -> none  [shards(): lax.all_to_all(frame_adjoint, 'rows', split_axis=2, concat_axis=0, tiled=...]
    ppermute x4 -> x0, waiting for transfers between devices: 15.8 us -> none  [the longest x2 8.87 us: extended(): lax.ppermute(lax.slice_in_dim(block, block.shape[dim] - width, None, axis...]
  transfers between devices with their start and end apart: 7 -> 0, of which waited for: 7 -> 0; matrix products, arithmetic and copies ran while one was open for 0% -> 0% of each run, Pallas kernels for 0% -> 0%
where the time goes in v2:
time: 81 us; the launch traced here: 80.9 us
  Pallas kernels  78.2 us (97%)
  local copies, waits for them, and re-layouts  1.96 us (2%)
    pallas_call x1, Pallas kernels, backward(): pl.pallas_call(kernel, out_shape=(jax.ShapeDtypeStruct((ROWS * GROUP, WID...  77.3 us
    unnamed x4, local copies, waits for them, and re-layouts  1.96 us

profile of v2, /device:TPU:8, one launch (start us, length us, event | category | flops | bytes accessed | tf_op | source)
XLA Modules:
  0.0 80.9 jit_solution(14134617718684428473)
XLA Ops:
  0.6 77.3 %shard_map.68 = (bf16[768,128]{1,0:T(8,128)(2,1)}, f32[32,32,128]{2,1,0:T(8,128)}) custom-call(s32[32]{0:T(128)} %slot.1, f32[24]{0:T(128)} %gain.1, bf16[768,128]{1,0:T(8,128)(2,1)} %bitcast.7, bf16[768,128]{1,0:T(8,128)(2,1)} %bitcast.8, bf16[27,24,192]{2,1,0:T(8,128)(2,1)} %w.1), custom_call_target="tpu_custom_call" | custom-call | tf_op jit(solution)/shard_map/pallas_call | solution.py:427
  77.9 0.0 copy-start
  77.9 1.0 %copy-done = f32[32,32,128]{2,1,0:T(8,128)S(1)} copy-done((f32[32,32,128]{2,1,0:T(8,128)S(1)}, f32[32,32,128]{2,1,0:T(8,128)}, u32[]{:S(2)}) %copy-start) | copy-done | bytes 524312
  79.0 0.0 copy-start.1
  79.0 0.9 %copy-done.1 = bf16[768,128]{1,0:T(8,128)(2,1)S(1)} copy-done((bf16[768,128]{1,0:T(8,128)(2,1)S(1)}, bf16[768,128]{1,0:T(8,128)(2,1)}, u32[]{:S(2)}) %copy-start.1) | copy-done | bytes 196632
  79.9 0.9 %shard_map.69 = (bf16[768,128]{1,0:T(8,128)(2,1)}, f32[27,24,192]{2,1,0:T(8,128)}) custom-call(bf16[768,128]{1,0:T(8,128)(2,1)S(1)} %copy-done.1, f32[1024,128]{1,0:T(8,128)S(1)} %bitcast.6), custom_call_target="tpu_custom_call" | custom-call | tf_op jit(solution)/shard_map/pallas_call | solution.py:482
Async XLA Ops:
  77.9 1.0 %copy-start = (f32[32,32,128]{2,1,0:T(8,128)S(1)}, f32[32,32,128]{2,1,0:T(8,128)}, u32[]{:S(2)}) copy-start(f32[32,32,128]{2,1,0:T(8,128)} %get-tuple-element.7) | copy-start | bytes 1572868
  79.0 0.9 %copy-start.1 = (bf16[768,128]{1,0:T(8,128)(2,1)S(1)}, bf16[768,128]{1,0:T(8,128)(2,1)}, u32[]{:S(2)}) copy-start(bf16[768,128]{1,0:T(8,128)(2,1)} %get-tuple-element.6.x_in) | copy-start | bytes 589828

commit v3 on v2

v3 whole, which is shorter than its diff:
```python
import jax
import jax.numpy as jnp
from jax import lax
from jax.experimental import pallas as pl
from jax.experimental.pallas import tpu as pltpu
from jax.sharding import PartitionSpec as P

CHANNELS = 192
GROUP = 24
WIDTH = 128
ROWS = 32
CHAN = 8
HALF = 4
RING = 4
PLANE = 16
TAPS = 27
PADDED = 32
FRAMES = 10
BLOCK = FRAMES * GROUP
SLAB = 72
KBLOCK = 224
PACK = 1024
LOW = 3 * KBLOCK
PIECE = PACK // ROWS
SLICE = PACK // RING
SHARE = PACK // PLANE
EPSILON = 1e-06
MESH = pl.DeviceIdType.MESH
VMEM_LIMIT = 56 * 1024 * 1024


def owner_of(row):
    return lax.rem(row, PLANE) * 2 + row // PLANE


def row_of(rows_index):
    return lax.rem(rows_index, 2) * PLANE + rows_index // 2


def greet_all(r, c):
    barrier = pltpu.get_barrier_semaphore()

    def tell(rows_index, chan_index):
        pl.semaphore_signal(
            barrier, inc=1, device_id=(rows_index, chan_index), device_id_type=MESH
        )

    def chan_step(d):
        chan_index = lax.rem(c + d, CHAN)
        tell(r, chan_index)
        tell(owner_of(r), chan_index)
        tell(row_of(r), chan_index)

    loop(1, ROWS, lambda d: tell(lax.rem(r + d, ROWS), c))
    loop(1, CHAN, chan_step)
    loop(1, HALF, lambda d: tell(r + 1 - 2 * lax.rem(r, 2), lax.rem(c + 2 * d, CHAN)))
    return barrier, ROWS - 1 + 3 * (CHAN - 1) + HALF - 1


def send(src, dst, send_sem, recv_sem, device):
    pltpu.make_async_remote_copy(
        src_ref=src,
        dst_ref=dst,
        send_sem=send_sem,
        recv_sem=recv_sem,
        device_id=device,
        device_id_type=MESH,
    ).start()


def drain(ref, sem):
    pltpu.make_async_copy(ref, ref, sem).wait()


def loop(low, high, step):
    def body(i, carry):
        step(i)
        return carry

    lax.fori_loop(low, high, body, 0)


def norm_of(values, gain):
    squares = jnp.sum(values * values, axis=0, keepdims=True)
    scale = lax.rsqrt(squares / CHANNELS + EPSILON)
    return scale, values * scale * gain


def sigmoid(v):
    return 1.0 / (1.0 + jnp.exp(-v))


def pair_lanes(low):
    return jnp.concatenate([low[: KBLOCK // 2], low[KBLOCK // 2 :]], axis=1)


def kernel(
    slot,
    gain,
    frames,
    x,
    w,
    x_grad,
    w_grad,
    wide,
    inverse,
    win,
    recv,
    ordered,
    adj,
    beside,
    x_all,
    gain_all,
    w_all,
    w_turned,
    stack,
    hidden,
    part,
    part_in,
    grad,
    grad_in,
    staged,
    red,
    red_in,
    final,
    win_s,
    win_r,
    x_s,
    x_r,
    gain_s,
    gain_r,
    core_s,
    core_r,
    w_s,
    w_r,
    a_s,
    a_r,
    after_s,
    before_s,
    beside_r,
    grad_s,
    grad_r,
    part_s,
    part_r,
    out_s,
    out_r,
    red_s,
    red_r,
    fin_s,
    fin_r,
    local,
):
    r = lax.axis_index("rows")
    c = lax.axis_index("chan")
    h = c // 2
    k = lax.rem(c, 2)
    z_low = lax.rem(r, 2)
    place = r // 2
    chip_x = r // 8
    row = row_of(r)
    owner = owner_of(r)
    at_home = row == r
    other = {"chan": c + 1 - 2 * k}

    barrier, greetings = greet_all(r, c)

    wide[...] = frames[...].astype(jnp.float32)
    empty = jnp.zeros((PADDED - GROUP, WIDTH), jnp.float32)

    def win_build(i):
        rows = wide[pl.ds(i, GROUP, stride=ROWS), :]
        win[owner_of(i)] = jnp.concatenate([rows, empty], axis=0).astype(jnp.bfloat16)

    loop(0, ROWS, win_build)
    recv[r] = win[r]
    gain_all[k, 0] = jnp.concatenate(
        [jnp.full((1, WIDTH), gain[j], jnp.float32) for j in range(GROUP)], axis=0
    )
    ordered[pl.ds(32 * GROUP, 2 * GROUP), :] = jnp.zeros((2 * GROUP, WIDTH), jnp.bfloat16)

    for col in range(3):
        rows = [w[9 * a + 3 * b + col].astype(jnp.float32) for a in range(3) for b in range(3)]
        rows = jnp.concatenate(
            rows + [jnp.zeros((KBLOCK - 3 * SLAB, CHANNELS), jnp.float32)], axis=0
        )
        w_all[0, KBLOCK * col : KBLOCK * (col + 1), :] = rows[:, :WIDTH].astype(jnp.bfloat16)
        begin = LOW + KBLOCK // 2 * col
        w_all[0, begin : begin + KBLOCK // 2, :] = pair_lanes(rows[:, WIDTH:]).astype(jnp.bfloat16)
    w_all[0, PACK - 16 :, :] = jnp.zeros((16, WIDTH), jnp.bfloat16)

    pl.semaphore_wait(barrier, greetings)

    mine_w = pl.ds(pl.multiple_of(SHARE * place, SHARE), SHARE)
    along_x = pl.ds(pl.multiple_of(SLICE * chip_x, SLICE), SLICE)

    def w_send(d):
        target = lax.rem(c + 2 * d, CHAN)
        send(w_all.at[0, mine_w], w_all.at[HALF - d, mine_w], w_s.at[0], w_r.at[0], {"chan": target})

    def w_spread_y(d):
        block = w_all.at[pl.ds(1, HALF - 1), mine_w]
        target = chip_x * 8 + lax.rem(lax.rem(r, 8) + 2 * d, 8)
        send(block, block, w_s.at[1], w_r.at[1], {"rows": target})

    def w_spread_x(d):
        block = w_all.at[pl.ds(1, HALF - 1), along_x]
        target = lax.rem(chip_x + d, RING) * 8 + lax.rem(r, 8)
        send(block, block, w_s.at[2], w_r.at[2], {"rows": target})

    def win_send(d):
        target = lax.rem(r + d, ROWS)
        send(win.at[target], recv.at[r], win_s, win_r, {"rows": target})

    loop(1, HALF, w_send)
    loop(1, ROWS, win_send)

    def x_send(d):
        target = lax.rem(c + 2 * d, CHAN)
        begin = pl.multiple_of((target // 2) * 192, 64)
        send(
            x.at[pl.ds(begin, 192)],
            x_all.at[k, lax.rem(HALF - d, HALF)],
            x_s,
            x_r,
            (owner, target),
        )

    def gain_send(d):
        target = lax.rem(c + 2 * d, CHAN)
        send(gain_all.at[k, 0], gain_all.at[k, HALF - d], gain_s, gain_r, {"chan": target})

    @pl.when(at_home)
    def _():
        begin = pl.multiple_of(h * 192, 64)
        pltpu.make_async_copy(x.at[pl.ds(begin, 192)], x_all.at[k, 0], x_r).start()

    @pl.when(jnp.logical_not(at_home))
    def _():
        x_send(0)

    loop(1, HALF, x_send)
    loop(1, HALF, gain_send)

    def invert(t):
        found = jnp.int32(0)
        for j in range(ROWS):
            found = jnp.where(slot[j] == t, j, found)
        inverse[t] = found

    loop(0, ROWS, invert)
    drain(w_all.at[pl.ds(1, HALF - 1), pl.ds(0, SHARE)], w_r.at[0])
    loop(1, RING, w_spread_y)
    drain(recv.at[pl.ds(0, ROWS - 1)], win_r)

    def order_step(p):
        low = recv[inverse[2 * p]].astype(jnp.float32)[:GROUP]
        high = recv[inverse[2 * p + 1]].astype(jnp.float32)[:GROUP]
        both = jnp.concatenate([low, high], axis=0).astype(jnp.bfloat16)
        ordered[pl.ds(pl.multiple_of(p * 2 * GROUP, 2 * GROUP), 2 * GROUP), :] = both

    loop(0, ROWS // 2, order_step)

    def a_send(d):
        target = lax.rem(c + 2 * d, CHAN)
        start = pl.multiple_of((target // 2) * (8 * GROUP), 64)
        send(
            ordered.at[pl.ds(start, BLOCK)],
            adj.at[HALF - d],
            a_s,
            a_r.at[HALF - d],
            {"chan": target},
        )

    for d in (1, 3, 2):
        a_send(d)
    adj[0] = ordered[pl.ds(pl.multiple_of(h * (8 * GROUP), 64), BLOCK), :]
    has_after = row < ROWS - 1
    has_before = row > 0

    @pl.when(jnp.logical_not(has_after))
    def _():
        beside[0] = jnp.zeros((HALF, BLOCK, WIDTH), jnp.bfloat16)

    @pl.when(jnp.logical_not(has_before))
    def _():
        beside[1] = jnp.zeros((HALF, BLOCK, WIDTH), jnp.bfloat16)

    def beside_send(d):
        @pl.when(has_after)
        def _():
            target = {"rows": owner_of(row + 1)}
            send(adj.at[d], beside.at[1, d], after_s, beside_r.at[1, d], target)

        @pl.when(has_before)
        def _():
            target = {"rows": owner_of(row - 1)}
            send(adj.at[d], beside.at[0, d], before_s, beside_r.at[0, d], target)

    def beside_wait(d):
        @pl.when(has_after)
        def _():
            drain(beside.at[0, d], beside_r.at[0, d])

        @pl.when(has_before)
        def _():
            drain(beside.at[1, d], beside_r.at[1, d])

    beside_send(0)

    drain(w_all.at[pl.ds(1, HALF - 1), pl.ds(0, 3 * SHARE)], w_r.at[1])
    loop(1, RING, w_spread_x)

    drain(x_all.at[k], x_r)
    drain(gain_all.at[k, pl.ds(1, HALF - 1)], gain_r)
    send(x_all.at[k], x_all.at[k], core_s.at[0], core_r.at[0], other)
    send(gain_all.at[k], gain_all.at[k], core_s.at[1], core_r.at[1], other)

    for d in (1, 3):
        drain(adj.at[d], a_r.at[d])
        beside_send(d)

    drain(x_all.at[1 - k], core_r.at[0])
    drain(gain_all.at[1 - k], core_r.at[1])

    def block_of(channel_group):
        return channel_group % 2, lax.rem(channel_group // 2 - h + HALF, HALF)

    gains = jnp.concatenate([gain_all[block_of(g)] for g in range(CHAN)], axis=0)
    for f in range(8):
        values = jnp.concatenate(
            [
                x_all[block_of(g)].astype(jnp.float32)[GROUP * f : GROUP * f + GROUP]
                for g in range(CHAN)
            ],
            axis=0,
        )
        _, normed = norm_of(values, gains)
        turned = jnp.transpose(normed * sigmoid(normed))
        hidden[WIDTH * f : WIDTH * (f + 1), :] = turned.astype(jnp.bfloat16)

    drain(adj.at[2], a_r.at[2])
    beside_send(2)

    lane = lax.broadcasted_iota(jnp.int32, (BLOCK, WIDTH), 1)

    def stack_step(d):
        three = [beside[0, d], adj[d], beside[1, d]]
        three = [v.astype(jnp.float32) for v in three]
        filler = jnp.zeros((KBLOCK - 3 * SLAB, WIDTH), jnp.float32)
        for col in range(3):
            if col == 0:
                moved = [
                    jnp.where(lane == WIDTH - 1, 0.0, pltpu.roll(v, WIDTH - 1, 1)) for v in three
                ]
            elif col == 1:
                moved = three
            else:
                moved = [jnp.where(lane == 0, 0.0, pltpu.roll(v, 1, 1)) for v in three]
            for f in range(8):
                slab = jnp.concatenate(
                    [
                        moved[b][GROUP * (f + 2 - a) : GROUP * (f + 3 - a)]
                        for a in range(3)
                        for b in range(3)
                    ]
                    + [filler],
                    axis=0,
                )
                stack[d, KBLOCK * col : KBLOCK * (col + 1), WIDTH * f : WIDTH * (f + 1)] = (
                    slab.astype(jnp.bfloat16)
                )

    def grad_step(d):
        sums = jnp.dot(stack[d], hidden[...], preferred_element_type=jnp.float32)
        grad[d, :LOW, :] = sums[:, :WIDTH].astype(jnp.bfloat16)
        for col in range(3):
            begin = LOW + KBLOCK // 2 * col
            low = sums[KBLOCK * col : KBLOCK * (col + 1), WIDTH:]
            grad[d, begin : begin + KBLOCK // 2, :] = pair_lanes(low).astype(jnp.bfloat16)
        grad[d, PACK - 16 :, :] = jnp.zeros((16, WIDTH), jnp.bfloat16)
        grad_in[d, place] = grad[d, pl.ds(pl.multiple_of(place * SHARE, SHARE), SHARE), :]

        def grad_send(e):
            target = lax.rem(place + e, PLANE)
            rows = pl.ds(pl.multiple_of(target * SHARE, SHARE), SHARE)
            send(
                grad.at[d, rows],
                grad_in.at[d, place],
                grad_s,
                grad_r.at[d],
                {"rows": target * 2 + z_low},
            )

        loop(1, PLANE, grad_send)

    def turn_weights(d):
        blocks = []
        for col in range(3):
            top = w_all[d, KBLOCK * col : KBLOCK * (col + 1), :].astype(jnp.float32)
            begin = LOW + KBLOCK // 2 * col
            low = w_all[d, begin : begin + KBLOCK // 2, :].astype(jnp.float32)
            low = jnp.concatenate([low, pltpu.roll(low, 64, 1)], axis=0)
            blocks.append((top, low))
        top = jnp.transpose(jnp.concatenate([b[0] for b in blocks], axis=0))
        low = jnp.transpose(jnp.concatenate([b[1] for b in blocks], axis=0))
        w_turned[d, :WIDTH, :] = top.astype(jnp.bfloat16)
        w_turned[d, WIDTH:, :] = low[:64].astype(jnp.bfloat16)

    def part_step(p):
        pixels = pl.ds(pl.multiple_of(p * 256, 256), 256)
        total = None
        for d in range(HALF):
            term = jnp.dot(w_turned[d], stack[d, :, pixels], preferred_element_type=jnp.float32)
            total = term if total is None else total + term
        part[2 * p] = total[:, :WIDTH]
        part[2 * p + 1] = total[:, WIDTH:]

    for d in (0, 1, 3, 2):
        beside_wait(d)
        stack_step(d)
        grad_step(d)
        if d == 0:
            turn_weights(0)
    drain(w_all.at[pl.ds(1, HALF - 1), pl.ds(0, 3 * SLICE)], w_r.at[2])
    loop(1, HALF, turn_weights)
    loop(2 * (1 - k), 2 * (1 - k) + 2, part_step)
    send(part.at[pl.ds(4 * (1 - k), 4)], part_in, part_s, part_r, other)
    loop(2 * k, 2 * k + 2, part_step)

    def reduce_step(d):
        drain(grad_in.at[d, pl.ds(0, PLANE - 1)], grad_r.at[d])

        def add_step(i, total):
            return total + grad_in[d, i].astype(jnp.float32)

        red[d] = lax.fori_loop(0, PLANE, add_step, jnp.zeros((SHARE, WIDTH), jnp.float32))

    reduce_step(0)
    mine = [
        x_all[block_of(g) + (pl.ds(pl.multiple_of(k * 96, 32), 96),)].astype(jnp.float32)
        for g in range(CHAN)
    ]
    drain(part_in, part_r)
    results = []
    for f in range(4):
        values = jnp.concatenate([m[GROUP * f : GROUP * f + GROUP] for m in mine], axis=0)
        scale, normed = norm_of(values, gains)
        s = sigmoid(normed)
        adjoint = part[4 * k + f] + part_in[f]
        normed_adjoint = adjoint * s * (1.0 + normed * (1.0 - s)) * gains
        projection = jnp.sum(normed_adjoint * values, axis=0, keepdims=True)
        results.append(
            scale * normed_adjoint - values * (scale * scale * scale * projection / CHANNELS)
        )
    for g in range(CHAN):
        rows = jnp.concatenate([y[GROUP * g : GROUP * g + GROUP] for y in results], axis=0)
        staged[g] = rows.astype(jnp.bfloat16)

    mine_out = pl.ds(pl.multiple_of(c * 96, 32), 96)

    def out_send(d):
        target = lax.rem(c + d, CHAN)
        send(staged.at[target], x_grad.at[mine_out], out_s, out_r, (row, target))

    @pl.when(at_home)
    def _():
        pltpu.make_async_copy(staged.at[c], x_grad.at[mine_out], out_r).start()

    @pl.when(jnp.logical_not(at_home))
    def _():
        out_send(0)

    loop(1, CHAN, out_send)

    for d in (1, 3, 2):
        reduce_step(d)
    red_in[z_low * HALF] = red[0, pl.ds(pl.multiple_of(z_low * PIECE, PIECE), PIECE), :]

    def red_send(d, chip_z):
        rows = pl.ds(pl.multiple_of(chip_z * PIECE, PIECE), PIECE)
        send(
            red.at[d, rows],
            red_in.at[z_low * HALF + lax.rem(HALF - d, HALF)],
            red_s,
            red_r,
            (r - z_low + chip_z, lax.rem(c + 2 * d, CHAN)),
        )

    loop(1, HALF, lambda d: red_send(d, z_low))
    loop(0, HALF, lambda d: red_send(d, 1 - z_low))
    drain(red_in.at[pl.ds(0, CHAN - 1)], red_r)
    whole = jnp.zeros((PIECE, WIDTH), jnp.float32)
    for i in range(CHAN):
        whole = whole + red_in[i]
    final[...] = whole * float(ROWS * ROWS * WIDTH) ** (-0.5)

    def final_send(d):
        send(final, w_grad.at[r], fin_s, fin_r, {"rows": lax.rem(r + d, ROWS)})

    loop(1, ROWS, final_send)
    own_final = pltpu.make_async_copy(final, w_grad.at[r], local)
    own_final.start()

    drain(win.at[pl.ds(0, ROWS - 1)], win_s)
    drain(gain_all.at[k, pl.ds(1, HALF - 1)], gain_s)
    drain(x_all.at[k], core_s.at[0])
    drain(gain_all.at[k], core_s.at[1])
    drain(w_all.at[pl.ds(1, HALF - 1), pl.ds(0, SHARE)], w_s.at[0])
    drain(w_all.at[pl.ds(1, HALF - 1), pl.ds(0, 3 * SHARE)], w_s.at[1])
    drain(w_all.at[pl.ds(1, HALF - 1), pl.ds(0, 3 * SLICE)], w_s.at[2])
    drain(adj.at[pl.ds(1, HALF - 1)], a_s)

    @pl.when(has_after)
    def _():
        drain(adj, after_s)

    @pl.when(has_before)
    def _():
        drain(adj, before_s)

    drain(grad_in.at[:, pl.ds(0, PLANE - 1)], grad_s)
    drain(part_in, part_s)

    @pl.when(at_home)
    def _():
        drain(x_all.at[k, pl.ds(1, HALF - 1)], x_s)
        drain(staged.at[pl.ds(0, CHAN - 1)], out_s)

    @pl.when(jnp.logical_not(at_home))
    def _():
        drain(x_all.at[k], x_s)
        drain(staged, out_s)

    drain(red_in.at[pl.ds(0, CHAN - 1)], red_s)
    drain(w_grad.at[pl.ds(0, ROWS - 1)], fin_s)
    own_final.wait()
    drain(x_grad, out_r)
    drain(w_grad.at[pl.ds(0, ROWS - 1)], fin_r)


def backward(slot, gain, frames, x, w):
    anywhere = pl.BlockSpec(memory_space=pl.ANY)
    scalars = pl.BlockSpec(memory_space=pltpu.SMEM)
    vmem = pl.BlockSpec(memory_space=pltpu.VMEM)
    bf16, f32 = jnp.bfloat16, jnp.float32
    one = pltpu.SemaphoreType.DMA
    many = lambda n: pltpu.SemaphoreType.DMA((n,))
    return pl.pallas_call(
        kernel,
        out_shape=(
            jax.ShapeDtypeStruct((ROWS * GROUP, WIDTH), bf16),
            jax.ShapeDtypeStruct((ROWS, PIECE, WIDTH), f32),
        ),
        in_specs=[scalars, scalars, vmem, vmem, vmem],
        out_specs=(anywhere, anywhere),
        scratch_shapes=[
            pltpu.VMEM((GROUP * ROWS, WIDTH), f32),
            pltpu.SMEM((ROWS,), jnp.int32),
            pltpu.VMEM((ROWS, PADDED, WIDTH), bf16),
            pltpu.VMEM((ROWS, PADDED, WIDTH), bf16),
            pltpu.VMEM((34 * GROUP, WIDTH), bf16),
            pltpu.VMEM((HALF, BLOCK, WIDTH), bf16),
            pltpu.VMEM((2, HALF, BLOCK, WIDTH), bf16),
            pltpu.VMEM((2, HALF, 8 * GROUP, WIDTH), bf16),
            pltpu.VMEM((2, HALF, GROUP, WIDTH), f32),
            pltpu.VMEM((HALF, PACK, WIDTH), bf16),
            pltpu.VMEM((HALF, CHANNELS, LOW), bf16),
            pltpu.VMEM((HALF, LOW, 8 * WIDTH), bf16),
            pltpu.VMEM((8 * WIDTH, CHANNELS), bf16),
            pltpu.VMEM((8, CHANNELS, WIDTH), f32),
            pltpu.VMEM((4, CHANNELS, WIDTH), f32),
            pltpu.VMEM((HALF, PACK, WIDTH), bf16),
            pltpu.VMEM((HALF, PLANE, SHARE, WIDTH), bf16),
            pltpu.VMEM((CHAN, 4 * GROUP, WIDTH), bf16),
            pltpu.VMEM((HALF, SHARE, WIDTH), f32),
            pltpu.VMEM((CHAN, PIECE, WIDTH), f32),
            pltpu.VMEM((PIECE, WIDTH), f32),
            one, one, one, one, one, one,
            many(2), many(2),
            many(3), many(3),
            one, many(HALF),
            one, one, pltpu.SemaphoreType.DMA((2, HALF)),
            one, many(HALF),
            one, one, one, one, one, one, one, one,
            one,
        ],
        compiler_params=pltpu.CompilerParams(
            collective_id=0, has_side_effects=True, vmem_limit_bytes=VMEM_LIMIT
        ),
    )(slot, gain, frames, x, w)


def unpack_kernel(x_in, w_in, x_out, w_out, held_x, held_w, sems):
    x_copy = pltpu.make_async_copy(x_in, held_x, sems.at[0])
    w_copy = pltpu.make_async_copy(w_in, held_w, sems.at[1])
    w_copy.start()
    x_copy.start()
    x_copy.wait()
    x_back = pltpu.make_async_copy(held_x, x_out, sems.at[2])
    x_back.start()
    w_copy.wait()
    for col in range(3):
        low = held_w[LOW + KBLOCK // 2 * col : LOW + KBLOCK // 2 * (col + 1), :]
        low = low.astype(jnp.float32)
        low = jnp.concatenate([low, pltpu.roll(low, 64, 1)], axis=0)
        top = held_w[KBLOCK * col : KBLOCK * (col + 1), :].astype(jnp.float32)
        for a in range(3):
            for b in range(3):
                begin = SLAB * a + GROUP * b
                w_out[9 * a + 3 * b + col, :, :WIDTH] = top[begin : begin + GROUP]
                w_out[9 * a + 3 * b + col, :, WIDTH:] = low[begin : begin + GROUP, :64]
    x_back.wait()


def unpack(x, w):
    anywhere = pl.BlockSpec(memory_space=pl.ANY)
    return pl.pallas_call(
        unpack_kernel,
        out_shape=(
            jax.ShapeDtypeStruct((ROWS * GROUP, WIDTH), jnp.bfloat16),
            jax.ShapeDtypeStruct((TAPS, GROUP, CHANNELS), jnp.float32),
        ),
        in_specs=[anywhere] * 2,
        out_specs=(anywhere, pl.BlockSpec(memory_space=pltpu.VMEM)),
        scratch_shapes=[
            pltpu.VMEM(x.shape, x.dtype),
            pltpu.VMEM(w.shape, w.dtype),
            pltpu.SemaphoreType.DMA((3,)),
        ],
        compiler_params=pltpu.CompilerParams(vmem_limit_bytes=VMEM_LIMIT),
    )(x, w)


def shards(frame_adjoint, frame_slot, inputs, gain, weight):
    frames = frame_adjoint.reshape(GROUP * ROWS, WIDTH)
    values = inputs.reshape(ROWS * GROUP, WIDTH)
    x_grad, w_grad = backward(frame_slot, gain, frames, values, weight)
    input_adjoint, weight_adjoint = unpack(x_grad, w_grad.reshape(PACK, WIDTH))
    return input_adjoint.reshape(ROWS, GROUP, 1, WIDTH), weight_adjoint


def solution(mesh):
    in_specs = (
        P("rows", "chan", None, None),
        P(),
        P(None, "chan", "rows", None),
        P("chan"),
        P(None, "chan", None),
    )
    out_specs = (P(None, "chan", "rows", None), P(None, "chan", None))
    return jax.shard_map(shards, mesh=mesh, in_specs=in_specs, out_specs=out_specs, check_vma=False)
```

time: 81 us -> 75.7 us (0.935)
  Pallas kernels: 78.2 us -> 74.3 us
  local copies, waits for them, and re-layouts: 1.96 us -> 0 us
    pallas_call x1, Pallas kernels: 77.3 us -> 71.7 us  [backward(): pl.pallas_call(kernel, out_shape=(jax.ShapeDtypeStruct((ROWS * GROUP, WID...]
    unnamed x4 -> x0, local copies, waits for them, and re-layouts: 1.96 us -> none
    pallas_call x1, Pallas kernels: 0.95 us -> 2.62 us  [unpack(): pl.pallas_call(unpack_kernel, out_shape=(jax.ShapeDtypeStruct((ROWS * GRO...]
where the time goes in v3:
time: 75.7 us; the launch traced here: 74.9 us
  Pallas kernels  74.3 us (98%)
    pallas_call x1, Pallas kernels, backward(): pl.pallas_call(kernel, out_shape=(jax.ShapeDtypeStruct((ROWS * GROUP, WID...  71.7 us
    pallas_call x1, Pallas kernels, unpack(): pl.pallas_call(unpack_kernel, out_shape=(jax.ShapeDtypeStruct((ROWS * GRO...  2.62 us

profile of v3, /device:TPU:8, one launch (start us, length us, event | category | flops | bytes accessed | tf_op | source)
XLA Modules:
  0.0 74.9 jit_solution(13323447515365923151)
XLA Ops:
  0.6 71.7 %shard_map.68 = (bf16[768,128]{1,0:T(8,128)(2,1)}, f32[32,32,128]{2,1,0:T(8,128)}) custom-call(s32[32]{0:T(128)} %slot.1, f32[24]{0:T(128)} %gain.1, bf16[768,128]{1,0:T(8,128)(2,1)} %bitcast.7, bf16[768,128]{1,0:T(8,128)(2,1)} %bitcast.8, bf16[27,24,192]{2,1,0:T(8,128)(2,1)} %w.1), custom_call_target="tpu_custom_call" | custom-call | tf_op jit(solution)/shard_map/pallas_call | solution.py:548
  72.3 2.6 %shard_map.69 = (bf16[768,128]{1,0:T(8,128)(2,1)}, f32[27,24,192]{2,1,0:T(8,128)}) custom-call(bf16[768,128]{1,0:T(8,128)(2,1)} %get-tuple-element.6.x_in, f32[1024,128]{1,0:T(8,128)} %bitcast.6), custom_call_target="tpu_custom_call" | custom-call | tf_op jit(solution)/shard_map/pallas_call | solution.py:617

commit v4 on v3

--- a/solution.py
+++ b/solution.py
@@ -30,11 +30,7 @@
 
 
 def owner_of(row):
-    return lax.rem(row, PLANE) * 2 + row // PLANE
-
-
-def row_of(rows_index):
-    return lax.rem(rows_index, 2) * PLANE + rows_index // 2
+    return row + lax.rem(row % 8 // 2, 2) * (1 - 2 * lax.rem(row, 2))
 
 
 def greet_all(r, c):
@@ -48,13 +44,11 @@
     def chan_step(d):
         chan_index = lax.rem(c + d, CHAN)
         tell(r, chan_index)
-        tell(owner_of(r), chan_index)
-        tell(row_of(r), chan_index)
+        tell(r + 1 - 2 * lax.rem(r, 2), chan_index)
 
     loop(1, ROWS, lambda d: tell(lax.rem(r + d, ROWS), c))
     loop(1, CHAN, chan_step)
-    loop(1, HALF, lambda d: tell(r + 1 - 2 * lax.rem(r, 2), lax.rem(c + 2 * d, CHAN)))
-    return barrier, ROWS - 1 + 3 * (CHAN - 1) + HALF - 1
+    return barrier, ROWS - 1 + 2 * (CHAN - 1)
 
 
 def send(src, dst, send_sem, recv_sem, device):
@@ -97,11 +91,14 @@
 def kernel(
     slot,
     gain,
+    frames_in,
+    x_in,
+    w_in,
+    x_grad,
+    w_grad,
     frames,
     x,
     w,
-    x_grad,
-    w_grad,
     wide,
     inverse,
     win,
@@ -157,12 +154,18 @@
     z_low = lax.rem(r, 2)
     place = r // 2
     chip_x = r // 8
-    row = row_of(r)
-    owner = owner_of(r)
+    row = owner_of(r)
     at_home = row == r
     other = {"chan": c + 1 - 2 * k}
 
+    fetches = [
+        pltpu.make_async_copy(src, dst, local.at[i])
+        for i, (src, dst) in enumerate(((frames_in, frames), (w_in, w), (x_in, x)))
+    ]
+    for fetch in fetches:
+        fetch.start()
     barrier, greetings = greet_all(r, c)
+    fetches[0].wait()
 
     wide[...] = frames[...].astype(jnp.float32)
     empty = jnp.zeros((PADDED - GROUP, WIDTH), jnp.float32)
@@ -178,6 +181,7 @@
     )
     ordered[pl.ds(32 * GROUP, 2 * GROUP), :] = jnp.zeros((2 * GROUP, WIDTH), jnp.bfloat16)
 
+    fetches[1].wait()
     for col in range(3):
         rows = [w[9 * a + 3 * b + col].astype(jnp.float32) for a in range(3) for b in range(3)]
         rows = jnp.concatenate(
@@ -187,6 +191,7 @@
         begin = LOW + KBLOCK // 2 * col
         w_all[0, begin : begin + KBLOCK // 2, :] = pair_lanes(rows[:, WIDTH:]).astype(jnp.bfloat16)
     w_all[0, PACK - 16 :, :] = jnp.zeros((16, WIDTH), jnp.bfloat16)
+    fetches[2].wait()
 
     pl.semaphore_wait(barrier, greetings)
 
@@ -222,7 +227,7 @@
             x_all.at[k, lax.rem(HALF - d, HALF)],
             x_s,
             x_r,
-            (owner, target),
+            (row, target),
         )
 
     def gain_send(d):
@@ -314,10 +319,6 @@
     drain(gain_all.at[k, pl.ds(1, HALF - 1)], gain_r)
     send(x_all.at[k], x_all.at[k], core_s.at[0], core_r.at[0], other)
     send(gain_all.at[k], gain_all.at[k], core_s.at[1], core_r.at[1], other)
-
-    for d in (1, 3):
-        drain(adj.at[d], a_r.at[d])
-        beside_send(d)
 
     drain(x_all.at[1 - k], core_r.at[0])
     drain(gain_all.at[1 - k], core_r.at[1])
@@ -337,9 +338,6 @@
         _, normed = norm_of(values, gains)
         turned = jnp.transpose(normed * sigmoid(normed))
         hidden[WIDTH * f : WIDTH * (f + 1), :] = turned.astype(jnp.bfloat16)
-
-    drain(adj.at[2], a_r.at[2])
-    beside_send(2)
 
     lane = lax.broadcasted_iota(jnp.int32, (BLOCK, WIDTH), 1)
 
@@ -415,12 +413,17 @@
         part[2 * p] = total[:, :WIDTH]
         part[2 * p + 1] = total[:, WIDTH:]
 
-    for d in (0, 1, 3, 2):
+    beside_wait(0)
+    stack_step(0)
+    grad_step(0)
+    for d in (1, 3, 2):
+        drain(adj.at[d], a_r.at[d])
+        beside_send(d)
+    turn_weights(0)
+    for d in (1, 3, 2):
         beside_wait(d)
         stack_step(d)
         grad_step(d)
-        if d == 0:
-            turn_weights(0)
     drain(w_all.at[pl.ds(1, HALF - 1), pl.ds(0, 3 * SLICE)], w_r.at[2])
     loop(1, HALF, turn_weights)
     loop(2 * (1 - k), 2 * (1 - k) + 2, part_step)
@@ -456,22 +459,6 @@
         rows = jnp.concatenate([y[GROUP * g : GROUP * g + GROUP] for y in results], axis=0)
         staged[g] = rows.astype(jnp.bfloat16)
 
-    mine_out = pl.ds(pl.multiple_of(c * 96, 32), 96)
-
-    def out_send(d):
-        target = lax.rem(c + d, CHAN)
-        send(staged.at[target], x_grad.at[mine_out], out_s, out_r, (row, target))
-
-    @pl.when(at_home)
-    def _():
-        pltpu.make_async_copy(staged.at[c], x_grad.at[mine_out], out_r).start()
-
-    @pl.when(jnp.logical_not(at_home))
-    def _():
-        out_send(0)
-
-    loop(1, CHAN, out_send)
-
     for d in (1, 3, 2):
         reduce_step(d)
     red_in[z_low * HALF] = red[0, pl.ds(pl.multiple_of(z_low * PIECE, PIECE), PIECE), :]
@@ -488,17 +475,33 @@
 
     loop(1, HALF, lambda d: red_send(d, z_low))
     loop(0, HALF, lambda d: red_send(d, 1 - z_low))
+    mine_out = pl.ds(pl.multiple_of(c * 96, 32), 96)
+
+    def out_send(d):
+        target = lax.rem(c + d, CHAN)
+        send(staged.at[target], x_grad.at[mine_out], out_s, out_r, (row, target))
+
+    @pl.when(at_home)
+    def _():
+        pltpu.make_async_copy(staged.at[c], x_grad.at[mine_out], out_r).start()
+
+    @pl.when(jnp.logical_not(at_home))
+    def _():
+        out_send(0)
+
+    loop(1, CHAN, out_send)
+
     drain(red_in.at[pl.ds(0, CHAN - 1)], red_r)
     whole = jnp.zeros((PIECE, WIDTH), jnp.float32)
     for i in range(CHAN):
         whole = whole + red_in[i]
-    final[...] = whole * float(ROWS * ROWS * WIDTH) ** (-0.5)
+    final[...] = (whole * float(ROWS * ROWS * WIDTH) ** (-0.5)).astype(final.dtype)
 
     def final_send(d):
         send(final, w_grad.at[r], fin_s, fin_r, {"rows": lax.rem(r + d, ROWS)})
 
     loop(1, ROWS, final_send)
-    own_final = pltpu.make_async_copy(final, w_grad.at[r], local)
+    own_final = pltpu.make_async_copy(final, w_grad.at[r], local.at[3])
     own_final.start()
 
     drain(win.at[pl.ds(0, ROWS - 1)], win_s)
@@ -541,7 +544,6 @@
 def backward(slot, gain, frames, x, w):
     anywhere = pl.BlockSpec(memory_space=pl.ANY)
     scalars = pl.BlockSpec(memory_space=pltpu.SMEM)
-    vmem = pl.BlockSpec(memory_space=pltpu.VMEM)
     bf16, f32 = jnp.bfloat16, jnp.float32
     one = pltpu.SemaphoreType.DMA
     many = lambda n: pltpu.SemaphoreType.DMA((n,))
@@ -549,11 +551,14 @@
         kernel,
         out_shape=(
             jax.ShapeDtypeStruct((ROWS * GROUP, WIDTH), bf16),
-            jax.ShapeDtypeStruct((ROWS, PIECE, WIDTH), f32),
+            jax.ShapeDtypeStruct((ROWS, PIECE, WIDTH), bf16),
         ),
-        in_specs=[scalars, scalars, vmem, vmem, vmem],
+        in_specs=[scalars, scalars] + [anywhere] * 3,
         out_specs=(anywhere, anywhere),
         scratch_shapes=[
+            pltpu.VMEM(frames.shape, bf16),
+            pltpu.VMEM(x.shape, bf16),
+            pltpu.VMEM(w.shape, bf16),
             pltpu.VMEM((GROUP * ROWS, WIDTH), f32),
             pltpu.SMEM((ROWS,), jnp.int32),
             pltpu.VMEM((ROWS, PADDED, WIDTH), bf16),
@@ -574,7 +579,7 @@
             pltpu.VMEM((CHAN, 4 * GROUP, WIDTH), bf16),
             pltpu.VMEM((HALF, SHARE, WIDTH), f32),
             pltpu.VMEM((CHAN, PIECE, WIDTH), f32),
-            pltpu.VMEM((PIECE, WIDTH), f32),
+            pltpu.VMEM((PIECE, WIDTH), bf16),
             one, one, one, one, one, one,
             many(2), many(2),
             many(3), many(3),
@@ -582,7 +587,7 @@
             one, one, pltpu.SemaphoreType.DMA((2, HALF)),
             one, many(HALF),
             one, one, one, one, one, one, one, one,
-            one,
+            many(4),
         ],
         compiler_params=pltpu.CompilerParams(
             collective_id=0, has_side_effects=True, vmem_limit_bytes=VMEM_LIMIT

time: 75.7 us -> 66.6 us (0.88)
  Pallas kernels: 74.3 us -> 64.9 us
    pallas_call x1, Pallas kernels: 71.7 us -> 62.4 us  [backward(): pl.pallas_call(kernel, out_shape=(jax.ShapeDtypeStruct((ROWS * GROUP, WID...]
where the time goes in v4:
time: 66.6 us; the launch traced here: 65.6 us
  Pallas kernels  64.9 us (97%)
    pallas_call x1, Pallas kernels, backward(): pl.pallas_call(kernel, out_shape=(jax.ShapeDtypeStruct((ROWS * GROUP, WID...  62.4 us
    pallas_call x1, Pallas kernels, unpack(): pl.pallas_call(unpack_kernel, out_shape=(jax.ShapeDtypeStruct((ROWS * GRO...  2.55 us

profile of v4, /device:TPU:8, one launch (start us, length us, event | category | flops | bytes accessed | tf_op | source)
XLA Modules:
  0.0 65.6 jit_solution(9888467577648033019)
XLA Ops:
  0.6 62.4 %shard_map.68 = (bf16[768,128]{1,0:T(8,128)(2,1)}, bf16[32,32,128]{2,1,0:T(8,128)(2,1)}) custom-call(s32[32]{0:T(128)} %slot.1, f32[24]{0:T(128)} %gain.1, bf16[768,128]{1,0:T(8,128)(2,1)} %bitcast.7, bf16[768,128]{1,0:T(8,128)(2,1)} %bitcast.8, bf16[27,24,192]{2,1,0:T(8,128)(2,1)} %w_in.1), custom_call_target="tpu_custom_call" | custom-call | tf_op jit(solution)/shard_map/pallas_call | solution.py:550
  63.0 2.5 %shard_map.69 = (bf16[768,128]{1,0:T(8,128)(2,1)}, f32[27,24,192]{2,1,0:T(8,128)}) custom-call(bf16[768,128]{1,0:T(8,128)(2,1)} %get-tuple-element.6.x_in, bf16[1024,128]{1,0:T(8,128)(2,1)} %bitcast.6), custom_call_target="tpu_custom_call" | custom-call | tf_op jit(solution)/shard_map/pallas_call | solution.py:622

commit v5 on v4

--- a/solution.py
+++ b/solution.py
@@ -196,21 +196,15 @@
     pl.semaphore_wait(barrier, greetings)
 
     mine_w = pl.ds(pl.multiple_of(SHARE * place, SHARE), SHARE)
-    along_x = pl.ds(pl.multiple_of(SLICE * chip_x, SLICE), SLICE)
 
     def w_send(d):
         target = lax.rem(c + 2 * d, CHAN)
         send(w_all.at[0, mine_w], w_all.at[HALF - d, mine_w], w_s.at[0], w_r.at[0], {"chan": target})
 
-    def w_spread_y(d):
+    def w_spread(e):
         block = w_all.at[pl.ds(1, HALF - 1), mine_w]
-        target = chip_x * 8 + lax.rem(lax.rem(r, 8) + 2 * d, 8)
+        target = lax.rem(place + e, PLANE) * 2 + z_low
         send(block, block, w_s.at[1], w_r.at[1], {"rows": target})
-
-    def w_spread_x(d):
-        block = w_all.at[pl.ds(1, HALF - 1), along_x]
-        target = lax.rem(chip_x + d, RING) * 8 + lax.rem(r, 8)
-        send(block, block, w_s.at[2], w_r.at[2], {"rows": target})
 
     def win_send(d):
         target = lax.rem(r + d, ROWS)
@@ -254,7 +248,7 @@
 
     loop(0, ROWS, invert)
     drain(w_all.at[pl.ds(1, HALF - 1), pl.ds(0, SHARE)], w_r.at[0])
-    loop(1, RING, w_spread_y)
+    loop(1, PLANE, w_spread)
     drain(recv.at[pl.ds(0, ROWS - 1)], win_r)
 
     def order_step(p):
@@ -276,7 +270,7 @@
             {"chan": target},
         )
 
-    for d in (1, 3, 2):
+    for d in (1, 3):
         a_send(d)
     adj[0] = ordered[pl.ds(pl.multiple_of(h * (8 * GROUP), 64), BLOCK), :]
     has_after = row < ROWS - 1
@@ -312,14 +306,12 @@
 
     beside_send(0)
 
-    drain(w_all.at[pl.ds(1, HALF - 1), pl.ds(0, 3 * SHARE)], w_r.at[1])
-    loop(1, RING, w_spread_x)
-
     drain(x_all.at[k], x_r)
     drain(gain_all.at[k, pl.ds(1, HALF - 1)], gain_r)
     send(x_all.at[k], x_all.at[k], core_s.at[0], core_r.at[0], other)
     send(gain_all.at[k], gain_all.at[k], core_s.at[1], core_r.at[1], other)
 
+    a_send(2)
     drain(x_all.at[1 - k], core_r.at[0])
     drain(gain_all.at[1 - k], core_r.at[1])
 
@@ -413,23 +405,35 @@
         part[2 * p] = total[:, :WIDTH]
         part[2 * p + 1] = total[:, WIDTH:]
 
+    for d in (1, 3):
+        drain(adj.at[d], a_r.at[d])
+        beside_send(d)
     beside_wait(0)
     stack_step(0)
     grad_step(0)
-    for d in (1, 3, 2):
-        drain(adj.at[d], a_r.at[d])
-        beside_send(d)
+    drain(adj.at[2], a_r.at[2])
+    beside_send(2)
     turn_weights(0)
     for d in (1, 3, 2):
         beside_wait(d)
         stack_step(d)
         grad_step(d)
-    drain(w_all.at[pl.ds(1, HALF - 1), pl.ds(0, 3 * SLICE)], w_r.at[2])
+    drain(w_all.at[pl.ds(1, HALF - 1), pl.ds(0, 15 * SHARE)], w_r.at[1])
     loop(1, HALF, turn_weights)
     loop(2 * (1 - k), 2 * (1 - k) + 2, part_step)
     send(part.at[pl.ds(4 * (1 - k), 4)], part_in, part_s, part_r, other)
     loop(2 * k, 2 * k + 2, part_step)
 
+    def red_send(d, chip_z):
+        rows = pl.ds(pl.multiple_of(chip_z * PIECE, PIECE), PIECE)
+        send(
+            red.at[d, rows],
+            red_in.at[z_low * HALF + lax.rem(HALF - d, HALF)],
+            red_s,
+            red_r,
+            (r - z_low + chip_z, lax.rem(c + 2 * d, CHAN)),
+        )
+
     def reduce_step(d):
         drain(grad_in.at[d, pl.ds(0, PLANE - 1)], grad_r.at[d])
 
@@ -437,6 +441,9 @@
             return total + grad_in[d, i].astype(jnp.float32)
 
         red[d] = lax.fori_loop(0, PLANE, add_step, jnp.zeros((SHARE, WIDTH), jnp.float32))
+        red_send(d, 1 - z_low)
+        if d > 0:
+            red_send(d, z_low)
 
     reduce_step(0)
     mine = [
@@ -463,18 +470,6 @@
         reduce_step(d)
     red_in[z_low * HALF] = red[0, pl.ds(pl.multiple_of(z_low * PIECE, PIECE), PIECE), :]
 
-    def red_send(d, chip_z):
-        rows = pl.ds(pl.multiple_of(chip_z * PIECE, PIECE), PIECE)
-        send(
-            red.at[d, rows],
-            red_in.at[z_low * HALF + lax.rem(HALF - d, HALF)],
-            red_s,
-            red_r,
-            (r - z_low + chip_z, lax.rem(c + 2 * d, CHAN)),
-        )
-
-    loop(1, HALF, lambda d: red_send(d, z_low))
-    loop(0, HALF, lambda d: red_send(d, 1 - z_low))
     mine_out = pl.ds(pl.multiple_of(c * 96, 32), 96)
 
     def out_send(d):
@@ -509,8 +504,7 @@
     drain(x_all.at[k], core_s.at[0])
     drain(gain_all.at[k], core_s.at[1])
     drain(w_all.at[pl.ds(1, HALF - 1), pl.ds(0, SHARE)], w_s.at[0])
-    drain(w_all.at[pl.ds(1, HALF - 1), pl.ds(0, 3 * SHARE)], w_s.at[1])
-    drain(w_all.at[pl.ds(1, HALF - 1), pl.ds(0, 3 * SLICE)], w_s.at[2])
+    drain(w_all.at[pl.ds(1, HALF - 1), pl.ds(0, 15 * SHARE)], w_s.at[1])
     drain(adj.at[pl.ds(1, HALF - 1)], a_s)
 
     @pl.when(has_after)
@@ -582,7 +576,7 @@
             pltpu.VMEM((PIECE, WIDTH), bf16),
             one, one, one, one, one, one,
             many(2), many(2),
-            many(3), many(3),
+            many(2), many(2),
             one, many(HALF),
             one, one, pltpu.SemaphoreType.DMA((2, HALF)),
             one, many(HALF),

time: 66.6 us -> 62.4 us (0.937); the launches traced: 65.6 us -> 62.2 us
  Pallas kernels: 64.9 us -> 61.6 us
    pallas_call x1, Pallas kernels: 62.4 us -> 59 us  [backward(): pl.pallas_call(kernel, out_shape=(jax.ShapeDtypeStruct((ROWS * GROUP, WID...]
where the time goes in v5:
time: 62.4 us; the launch traced here: 62.2 us
  Pallas kernels  61.6 us (99%)
  between operations  0.64 us (1%)
    pallas_call x1, Pallas kernels, backward(): pl.pallas_call(kernel, out_shape=(jax.ShapeDtypeStruct((ROWS * GROUP, WID...  59 us
    pallas_call x1, Pallas kernels, unpack(): pl.pallas_call(unpack_kernel, out_shape=(jax.ShapeDtypeStruct((ROWS * GRO...  2.55 us

profile of v5, /device:TPU:8, one launch (start us, length us, event | category | flops | bytes accessed | tf_op | source)
XLA Modules:
  0.0 62.2 jit_solution(6833724795809565337)
XLA Ops:
  0.6 59.0 %shard_map.68 = (bf16[768,128]{1,0:T(8,128)(2,1)}, bf16[32,32,128]{2,1,0:T(8,128)(2,1)}) custom-call(s32[32]{0:T(128)} %slot.1, f32[24]{0:T(128)} %gain.1, bf16[768,128]{1,0:T(8,128)(2,1)} %bitcast.7, bf16[768,128]{1,0:T(8,128)(2,1)} %bitcast.8, bf16[27,24,192]{2,1,0:T(8,128)(2,1)} %w_in.1), custom_call_target="tpu_custom_call" | custom-call | tf_op jit(solution)/shard_map/pallas_call | solution.py:544
  59.6 2.5 %shard_map.69 = (bf16[768,128]{1,0:T(8,128)(2,1)}, f32[27,24,192]{2,1,0:T(8,128)}) custom-call(bf16[768,128]{1,0:T(8,128)(2,1)} %get-tuple-element.6.x_in, bf16[1024,128]{1,0:T(8,128)(2,1)} %bitcast.6), custom_call_target="tpu_custom_call" | custom-call | tf_op jit(solution)/shard_map/pallas_call | solution.py:616

commit v6 on v5

--- a/solution.py
+++ b/solution.py
@@ -89,13 +89,15 @@
 
 
 def kernel(
-    slot,
-    gain,
+    slot_in,
+    gain_in,
     frames_in,
     x_in,
     w_in,
     x_grad,
     w_grad,
+    slot,
+    gain,
     frames,
     x,
     w,
@@ -160,7 +162,9 @@
 
     fetches = [
         pltpu.make_async_copy(src, dst, local.at[i])
-        for i, (src, dst) in enumerate(((frames_in, frames), (w_in, w), (x_in, x)))
+        for i, (src, dst) in enumerate(
+            ((frames_in, frames), (w_in, w), (x_in, x), (gain_in, gain), (slot_in, slot))
+        )
     ]
     for fetch in fetches:
         fetch.start()
@@ -176,6 +180,7 @@
 
     loop(0, ROWS, win_build)
     recv[r] = win[r]
+    fetches[3].wait()
     gain_all[k, 0] = jnp.concatenate(
         [jnp.full((1, WIDTH), gain[j], jnp.float32) for j in range(GROUP)], axis=0
     )
@@ -192,6 +197,7 @@
         w_all[0, begin : begin + KBLOCK // 2, :] = pair_lanes(rows[:, WIDTH:]).astype(jnp.bfloat16)
     w_all[0, PACK - 16 :, :] = jnp.zeros((16, WIDTH), jnp.bfloat16)
     fetches[2].wait()
+    fetches[4].wait()
 
     pl.semaphore_wait(barrier, greetings)
 
@@ -311,7 +317,6 @@
     send(x_all.at[k], x_all.at[k], core_s.at[0], core_r.at[0], other)
     send(gain_all.at[k], gain_all.at[k], core_s.at[1], core_r.at[1], other)
 
-    a_send(2)
     drain(x_all.at[1 - k], core_r.at[0])
     drain(gain_all.at[1 - k], core_r.at[1])
 
@@ -405,6 +410,7 @@
         part[2 * p] = total[:, :WIDTH]
         part[2 * p + 1] = total[:, WIDTH:]
 
+    a_send(2)
     for d in (1, 3):
         drain(adj.at[d], a_r.at[d])
         beside_send(d)
@@ -446,6 +452,10 @@
             red_send(d, z_low)
 
     reduce_step(0)
+    for d in (1, 3, 2):
+        reduce_step(d)
+    red_in[z_low * HALF] = red[0, pl.ds(pl.multiple_of(z_low * PIECE, PIECE), PIECE), :]
+
     mine = [
         x_all[block_of(g) + (pl.ds(pl.multiple_of(k * 96, 32), 96),)].astype(jnp.float32)
         for g in range(CHAN)
@@ -466,10 +476,6 @@
         rows = jnp.concatenate([y[GROUP * g : GROUP * g + GROUP] for y in results], axis=0)
         staged[g] = rows.astype(jnp.bfloat16)
 
-    for d in (1, 3, 2):
-        reduce_step(d)
-    red_in[z_low * HALF] = red[0, pl.ds(pl.multiple_of(z_low * PIECE, PIECE), PIECE), :]
-
     mine_out = pl.ds(pl.multiple_of(c * 96, 32), 96)
 
     def out_send(d):
@@ -496,7 +502,7 @@
         send(final, w_grad.at[r], fin_s, fin_r, {"rows": lax.rem(r + d, ROWS)})
 
     loop(1, ROWS, final_send)
-    own_final = pltpu.make_async_copy(final, w_grad.at[r], local.at[3])
+    own_final = pltpu.make_async_copy(final, w_grad.at[r], local.at[5])
     own_final.start()
 
     drain(win.at[pl.ds(0, ROWS - 1)], win_s)
@@ -537,7 +543,6 @@
 
 def backward(slot, gain, frames, x, w):
     anywhere = pl.BlockSpec(memory_space=pl.ANY)
-    scalars = pl.BlockSpec(memory_space=pltpu.SMEM)
     bf16, f32 = jnp.bfloat16, jnp.float32
     one = pltpu.SemaphoreType.DMA
     many = lambda n: pltpu.SemaphoreType.DMA((n,))
@@ -547,9 +552,11 @@
             jax.ShapeDtypeStruct((ROWS * GROUP, WIDTH), bf16),
             jax.ShapeDtypeStruct((ROWS, PIECE, WIDTH), bf16),
         ),
-        in_specs=[scalars, scalars] + [anywhere] * 3,
+        in_specs=[anywhere] * 5,
         out_specs=(anywhere, anywhere),
         scratch_shapes=[
+            pltpu.SMEM(slot.shape, jnp.int32),
+            pltpu.SMEM(gain.shape, f32),
             pltpu.VMEM(frames.shape, bf16),
             pltpu.VMEM(x.shape, bf16),
             pltpu.VMEM(w.shape, bf16),
@@ -581,7 +588,7 @@
             one, one, pltpu.SemaphoreType.DMA((2, HALF)),
             one, many(HALF),
             one, one, one, one, one, one, one, one,
-            many(4),
+            many(6),
         ],
         compiler_params=pltpu.CompilerParams(
             collective_id=0, has_side_effects=True, vmem_limit_bytes=VMEM_LIMIT
@@ -589,26 +596,32 @@
     )(slot, gain, frames, x, w)
 
 
-def unpack_kernel(x_in, w_in, x_out, w_out, held_x, held_w, sems):
+def unpack_kernel(x_in, w_in, x_out, w_out, held_x, held_w, spread, sems):
     x_copy = pltpu.make_async_copy(x_in, held_x, sems.at[0])
     w_copy = pltpu.make_async_copy(w_in, held_w, sems.at[1])
     w_copy.start()
     x_copy.start()
-    x_copy.wait()
     x_back = pltpu.make_async_copy(held_x, x_out, sems.at[2])
-    x_back.start()
     w_copy.wait()
+    backs = []
     for col in range(3):
         low = held_w[LOW + KBLOCK // 2 * col : LOW + KBLOCK // 2 * (col + 1), :]
         low = low.astype(jnp.float32)
         low = jnp.concatenate([low, pltpu.roll(low, 64, 1)], axis=0)
         top = held_w[KBLOCK * col : KBLOCK * (col + 1), :].astype(jnp.float32)
-        for a in range(3):
-            for b in range(3):
-                begin = SLAB * a + GROUP * b
-                w_out[9 * a + 3 * b + col, :, :WIDTH] = top[begin : begin + GROUP]
-                w_out[9 * a + 3 * b + col, :, WIDTH:] = low[begin : begin + GROUP, :64]
+        for tap in range(9):
+            begin = GROUP * tap
+            spread[col, tap, :, :WIDTH] = top[begin : begin + GROUP]
+            spread[col, tap, :, WIDTH:] = low[begin : begin + GROUP, :64]
+        back = pltpu.make_async_copy(spread.at[col], w_out.at[:, col], sems.at[3 + col])
+        back.start()
+        backs.append(back)
+        if col == 0:
+            x_copy.wait()
+            x_back.start()
     x_back.wait()
+    for back in backs:
+        back.wait()
 
 
 def unpack(x, w):
@@ -617,14 +630,15 @@
         unpack_kernel,
         out_shape=(
             jax.ShapeDtypeStruct((ROWS * GROUP, WIDTH), jnp.bfloat16),
-            jax.ShapeDtypeStruct((TAPS, GROUP, CHANNELS), jnp.float32),
+            jax.ShapeDtypeStruct((9, 3, GROUP, CHANNELS), jnp.float32),
         ),
         in_specs=[anywhere] * 2,
-        out_specs=(anywhere, pl.BlockSpec(memory_space=pltpu.VMEM)),
+        out_specs=(anywhere, anywhere),
         scratch_shapes=[
             pltpu.VMEM(x.shape, x.dtype),
             pltpu.VMEM(w.shape, w.dtype),
-            pltpu.SemaphoreType.DMA((3,)),
+            pltpu.VMEM((3, 9, GROUP, CHANNELS), jnp.float32),
+            pltpu.SemaphoreType.DMA((6,)),
         ],
         compiler_params=pltpu.CompilerParams(vmem_limit_bytes=VMEM_LIMIT),
     )(x, w)
@@ -635,6 +649,7 @@
     values = inputs.reshape(ROWS * GROUP, WIDTH)
     x_grad, w_grad = backward(frame_slot, gain, frames, values, weight)
     input_adjoint, weight_adjoint = unpack(x_grad, w_grad.reshape(PACK, WIDTH))
+    weight_adjoint = weight_adjoint.reshape(TAPS, GROUP, CHANNELS)
     return input_adjoint.reshape(ROWS, GROUP, 1, WIDTH), weight_adjoint
 
 

time: 62.4 us -> 61 us (0.978)
  Pallas kernels: 61.6 us -> 59.7 us
    pallas_call x1, Pallas kernels: 59 us -> 57.7 us  [backward(): pl.pallas_call(kernel, out_shape=(jax.ShapeDtypeStruct((ROWS * GROUP, WID...]
where the time goes in v6:
time: 61 us; the launch traced here: 60.3 us
  Pallas kernels  59.7 us (98%)
  between operations  0.64 us (1%)
    pallas_call x1, Pallas kernels, backward(): pl.pallas_call(kernel, out_shape=(jax.ShapeDtypeStruct((ROWS * GROUP, WID...  57.7 us
    pallas_call x1, Pallas kernels, unpack(): pl.pallas_call(unpack_kernel, out_shape=(jax.ShapeDtypeStruct((ROWS * GRO...  1.97 us

profile of v6, /device:TPU:8, one launch (start us, length us, event | category | flops | bytes accessed | tf_op | source)
XLA Modules:
  0.0 60.3 jit_solution(14955364357781776981)
XLA Ops:
  0.6 57.7 %shard_map.68 = (bf16[768,128]{1,0:T(8,128)(2,1)}, bf16[32,32,128]{2,1,0:T(8,128)(2,1)}) custom-call(s32[32]{0:T(128)} %slot_in.1, f32[24]{0:T(128)} %gain_in.1, bf16[768,128]{1,0:T(8,128)(2,1)} %bitcast.8, bf16[768,128]{1,0:T(8,128)(2,1)} %bitcast.9, bf16[27,24,192]{2,1,0:T(8,128)(2,1)} %w_in.1), custom_call_target="tpu_custom_call" | custom-call | tf_op jit(solution)/shard_map/pallas_call | solution.py:549
  58.4 2.0 %shard_map.69 = (bf16[768,128]{1,0:T(8,128)(2,1)}, f32[9,3,24,192]{3,2,1,0:T(8,128)}) custom-call(bf16[768,128]{1,0:T(8,128)(2,1)} %get-tuple-element.6.x_in, bf16[1024,128]{1,0:T(8,128)(2,1)} %bitcast.7), custom_call_target="tpu_custom_call" | custom-call | tf_op jit(solution)/shard_map/pallas_call | solution.py:629

commit v7 on v6

--- a/solution.py
+++ b/solution.py
@@ -419,13 +419,12 @@
     grad_step(0)
     drain(adj.at[2], a_r.at[2])
     beside_send(2)
-    turn_weights(0)
     for d in (1, 3, 2):
         beside_wait(d)
         stack_step(d)
         grad_step(d)
     drain(w_all.at[pl.ds(1, HALF - 1), pl.ds(0, 15 * SHARE)], w_r.at[1])
-    loop(1, HALF, turn_weights)
+    loop(0, HALF, turn_weights)
     loop(2 * (1 - k), 2 * (1 - k) + 2, part_step)
     send(part.at[pl.ds(4 * (1 - k), 4)], part_in, part_s, part_r, other)
     loop(2 * k, 2 * k + 2, part_step)

time: 61 us -> 60.8 us (level)
  no operation moved by 1% of the time
where the time goes in v7:
time: 60.8 us; the launch traced here: 60.5 us
  Pallas kernels  59.8 us (98%)
  between operations  0.64 us (1%)
    pallas_call x1, Pallas kernels, backward(): pl.pallas_call(kernel, out_shape=(jax.ShapeDtypeStruct((ROWS * GROUP, WID...  57.8 us
    pallas_call x1, Pallas kernels, unpack(): pl.pallas_call(unpack_kernel, out_shape=(jax.ShapeDtypeStruct((ROWS * GRO...  1.97 us

profile of v7, /device:TPU:8, one launch (start us, length us, event | category | flops | bytes accessed | tf_op | source)
XLA Modules:
  0.0 60.5 jit_solution(10895963360931886738)
XLA Ops:
  0.6 57.8 %shard_map.68 = (bf16[768,128]{1,0:T(8,128)(2,1)}, bf16[32,32,128]{2,1,0:T(8,128)(2,1)}) custom-call(s32[32]{0:T(128)} %slot_in.1, f32[24]{0:T(128)} %gain_in.1, bf16[768,128]{1,0:T(8,128)(2,1)} %bitcast.8, bf16[768,128]{1,0:T(8,128)(2,1)} %bitcast.9, bf16[27,24,192]{2,1,0:T(8,128)(2,1)} %w_in.1), custom_call_target="tpu_custom_call" | custom-call | tf_op jit(solution)/shard_map/pallas_call | solution.py:548
  58.5 2.0 %shard_map.69 = (bf16[768,128]{1,0:T(8,128)(2,1)}, f32[9,3,24,192]{3,2,1,0:T(8,128)}) custom-call(bf16[768,128]{1,0:T(8,128)(2,1)} %get-tuple-element.6.x_in, bf16[1024,128]{1,0:T(8,128)(2,1)} %bitcast.7), custom_call_target="tpu_custom_call" | custom-call | tf_op jit(solution)/shard_map/pallas_call | solution.py:628

commit v8 on v7

--- a/solution.py
+++ b/solution.py
@@ -312,10 +312,10 @@
 
     beside_send(0)
 
+    drain(gain_all.at[k, pl.ds(1, HALF - 1)], gain_r)
+    send(gain_all.at[k], gain_all.at[k], core_s.at[1], core_r.at[1], other)
     drain(x_all.at[k], x_r)
-    drain(gain_all.at[k, pl.ds(1, HALF - 1)], gain_r)
     send(x_all.at[k], x_all.at[k], core_s.at[0], core_r.at[0], other)
-    send(gain_all.at[k], gain_all.at[k], core_s.at[1], core_r.at[1], other)
 
     drain(x_all.at[1 - k], core_r.at[0])
     drain(gain_all.at[1 - k], core_r.at[1])

time: 60.8 us -> 60.8 us (level)
  no operation moved by 1% of the time
where the time goes in v8:
time: 60.8 us; the launch traced here: 60.4 us
  Pallas kernels  59.7 us (98%)
  between operations  0.64 us (1%)
    pallas_call x1, Pallas kernels, backward(): pl.pallas_call(kernel, out_shape=(jax.ShapeDtypeStruct((ROWS * GROUP, WID...  57.7 us
    pallas_call x1, Pallas kernels, unpack(): pl.pallas_call(unpack_kernel, out_shape=(jax.ShapeDtypeStruct((ROWS * GRO...  1.97 us

profile of v8, /device:TPU:8, one launch (start us, length us, event | category | flops | bytes accessed | tf_op | source)
XLA Modules:
  0.0 60.4 jit_solution(10182629880435225393)
XLA Ops:
  0.6 57.7 %shard_map.68 = (bf16[768,128]{1,0:T(8,128)(2,1)}, bf16[32,32,128]{2,1,0:T(8,128)(2,1)}) custom-call(s32[32]{0:T(128)} %slot_in.1, f32[24]{0:T(128)} %gain_in.1, bf16[768,128]{1,0:T(8,128)(2,1)} %bitcast.8, bf16[768,128]{1,0:T(8,128)(2,1)} %bitcast.9, bf16[27,24,192]{2,1,0:T(8,128)(2,1)} %w_in.1), custom_call_target="tpu_custom_call" | custom-call | tf_op jit(solution)/shard_map/pallas_call | solution.py:548
  58.4 2.0 %shard_map.69 = (bf16[768,128]{1,0:T(8,128)(2,1)}, f32[9,3,24,192]{3,2,1,0:T(8,128)}) custom-call(bf16[768,128]{1,0:T(8,128)(2,1)} %get-tuple-element.6.x_in, bf16[1024,128]{1,0:T(8,128)(2,1)} %bitcast.7), custom_call_target="tpu_custom_call" | custom-call | tf_op jit(solution)/shard_map/pallas_call | solution.py:628
